TPU v7x, 32 devices: a whole 2x2x4 slice. The times are simulated.
32 devices in a mesh: region: 8 (over z, y), scen: 4 (over x, core).
Axes of the slice: x: 2, y: 2, z: 4, core: 2. Of those that a mesh axis runs over, the one named last changes fastest.
Arguments:
- inverse_blocks: float32 [256, 5, 96, 96], P('region')
- block_cols: int32 [256, 5], P('region'), may hold values from 0 to 31, as said below
- source_current: float32 [24576], P('region'), may hold values from -6 to 6
- node_decay: float32 [24576], P('region'), may hold values from 0.3 to 0.95
- node_gain: float32 [24576], P('region'), may hold values from 0.05 to 0.5
- voltage_init: float32 [256, 24576], P('scen', 'region'), may hold values from -6 to 6
- branch_init: float32 [256, 24576], P('scen', 'region'), may hold values from -3 to 3
- wave_init: float32 [8, 256, 2048], P(None, 'scen', 'region'), may hold values from -6 to 6
- line_node: int32 [2048], P('region'), may hold values from 0 to 3071
- line_delay: int32 [2048], P('region'), may hold values from 1 to 8, as said below
- line_admittance: float32 [2048], P('region'), may hold values from 0.19 to 1, as said below
- conv_region: int32 [3072, 1], P('region'), may hold values from 0 to 7; in each aligned block of 384 rows (0 to 383, 384 to 767, ...) at most 115 rows name the same one
- conv_node: int32 [3072], P('region'), may hold values from 0 to 3071
- conv_power: float32 [3072], P('region'), may hold values from 0.3 to 3
- conv_gains: float32 [2, 3072], P(None, 'region'), may hold values from 0.2 to 0.9
- conv_init: float32 [2, 256, 3072], P(None, 'scen', 'region'), may hold values from -3 to 3
- fault_node: int32 [256], P('scen'), may hold values from 0 to 24575
- fault_kind: int32 [256], P('scen'), may hold values from 0 to 3
Outputs:
- voltage: float32 [256, 24576], P('scen', 'region')
- branch_history: float32 [256, 24576], P('scen', 'region')
- wave_history: float32 [8, 256, 2048], P(None, 'scen', 'region')
- conv_state: float32 [2, 256, 3072], P(None, 'scen', 'region')
- envelope: float32 [24576], P('region')
Inputs may be any that keep to these rules, and one draw needn't show every extreme that they name: `block_cols`: entry 0 of row b is b mod 32; the 5 entries of a row are distinct. `line_delay`: entry r * 2 * 128 + l with l < 128 equals entry ((r - 1) mod 8) * 2 * 128 + 128 + l: both ends of a line have one delay. `line_admittance`: entry r * 2 * 128 + l with l < 128 equals entry ((r - 1) mod 8) * 2 * 128 + 128 + l: both ends of a line have one admittance. `conv_region`: among the converters of one region index of the mesh (aligned blocks of 384 rows), at most 115 lie in one region, and some region gets exactly 115.
All inputs are finite; a program needn't handle non-finite values.
Results may differ from a plain program's by a relative error of at most 0.00011.
Values sent between devices are 32-bit elements; how exact they have to be, the bound alone decides.
No kernel may reach another device: no remote copies, remote signals or barrier semaphores. Data moves between devices by JAX's collectives and lax.ppermute only.
A program may use at most 128 MiB of HBM per device.

v0:
```python
import functools
import math

import jax
import jax.numpy as jnp
from jax import lax
from jax.experimental import pallas as pl
from jax.experimental.pallas import tpu as pltpu
from jax.sharding import PartitionSpec as P

STEPS = 4
LANES = 128
BF = jnp.bfloat16
F32 = jnp.float32
I32 = jnp.int32
VMEM = pl.BlockSpec(memory_space=pltpu.VMEM)
SMEM = pl.BlockSpec(memory_space=pltpu.SMEM)
HBM = pl.BlockSpec(memory_space=pltpu.HBM)
PARAMS = pltpu.CompilerParams(vmem_limit_bytes=20 << 20)


def round_up(value, unit):
    return -(-value // unit) * unit


def iota(shape, dim):
    return lax.broadcasted_iota(I32, shape, dim)


def split_2(value):
    high = value.astype(BF)
    return high, (value - high.astype(F32)).astype(BF)


def split_3(value):
    high = value.astype(BF)
    rest = value - high.astype(F32)
    middle = rest.astype(BF)
    return high, middle, (rest - middle.astype(F32)).astype(BF)


def stacked(value):
    high, low = split_2(value)
    return jnp.concatenate([high, low], axis=0)


def folded(value):
    half = value.shape[0] // 2
    return value[:half] + value[half:]


def dot(left, right):
    return jnp.dot(left, right, preferred_element_type=F32)


def one_hot(mask):
    return jnp.where(mask, 1.0, 0.0).astype(BF)


def padded_index(nodes, width, padded):
    block = jnp.floor((nodes + 0.5) * (1.0 / width))
    return nodes + block * (padded - width)


class Sizes:
    def __init__(self, inverse_blocks, voltage, wave_init, line_node, conv_node):
        self.blocks, self.picks, self.width, _ = inverse_blocks.shape
        self.scen, self.nodes = voltage.shape
        self.delays = wave_init.shape[0]
        self.ends = line_node.shape[0]
        self.lines = self.ends // 2
        self.convs = conv_node.shape[0]
        self.regions = lax.axis_size("region")
        self.capacity = max(2, 12 * self.convs // (5 * self.regions))
        self.rows = round_up(self.capacity + 4, 8)
        self.slots = self.regions * self.rows
        self.slot_lanes = round_up(self.slots, LANES)
        self.padded = round_up(self.width, LANES)
        self.lanes = self.blocks * self.padded
        self.group = math.lcm(self.width, LANES) // self.width

    def vmem(self, shape, dtype=F32):
        return pltpu.VMEM(shape, dtype)


def pad_blocks(size, source, store):
    group_width = size.group * size.width
    for first in range(0, size.blocks, size.group):
        chunk = source[:, first * size.width : first * size.width + group_width]
        for j in range(size.group):
            part = chunk[:, j * size.width : (j + 1) * size.width]
            zeros = jnp.zeros((part.shape[0], size.padded - size.width), part.dtype)
            store(first + j, jnp.concatenate([part, zeros], axis=1))


def unpad_blocks(size, load, target):
    group_width = size.group * size.width
    for first in range(0, size.blocks, size.group):
        parts = [load(first + j)[:, : size.width] for j in range(size.group)]
        target[:, first * size.width : first * size.width + group_width] = jnp.concatenate(
            parts, axis=1
        )


def pack_kernel(size, region, node, power, gains, init, out, dst_out):
    convs, slots = size.convs, size.slots
    target = region[...]
    member = iota((round_up(size.regions, 16), convs), 0) == target
    before = one_hot(iota((convs, convs), 0) < iota((convs, convs), 1))
    earlier = dot(one_hot(member), before)
    rank = jnp.sum(jnp.where(member, earlier, 0.0), axis=0, keepdims=True)
    dst = target * size.rows + rank.astype(I32)
    dst_out[...] = dst
    select = one_hot(iota((slots, convs), 0) == dst)
    state = jnp.concatenate([init[0], init[1]], axis=0)
    settings = jnp.concatenate(
        [power[...], gains[...], node[...].astype(F32), jnp.zeros((LANES - 4, convs), F32)], axis=0
    )
    payload = jnp.concatenate([state.T, settings.T], axis=1)
    width = state.shape[0]
    rows = sum(dot(select, part) for part in split_3(payload))
    for r in range(size.regions):
        chunk = rows[r * size.rows : (r + 1) * size.rows]
        out[r] = chunk[:, :width]
        filler = jnp.zeros((LANES - size.rows, LANES), F32)
        turned = jnp.concatenate([chunk[:, width:], filler], axis=0).T
        out[r, size.capacity : size.capacity + 4, :] = turned[:4]


def converter_part(size, vb, cg, cs, prm, filt, amps, volt, branch, node_rows, peak, fault, base):
    measured = folded(dot(vb[...], cg[...]))
    filtered = filt[...]
    filtered = filtered + prm[2:3, :] * (measured - filtered)
    current = amps[...]
    target = prm[0:1, :] * filtered / (1.0 + filtered * filtered)
    current = current + prm[1:2, :] * (target - current)
    filt[...] = filtered
    amps[...] = current
    pair = stacked(current)
    site, level = fault
    lane = iota((size.scen, size.padded), 1)
    for b in range(size.blocks):
        injected = folded(dot(pair, cs[:, b * size.padded : (b + 1) * size.padded]))
        v = volt[b]
        history = node_rows[b, 1:2, :] * branch[b] + node_rows[b, 2:3, :] * v
        branch[b] = history
        hit = jnp.where(lane + b * size.padded == site, level, 0.0)
        base[b] = node_rows[b, 0:1, :] - history + injected - hit * v
        if peak is not None:
            size_of = jnp.abs(v)
            top = size_of[:8]
            for s in range(8, size.scen, 8):
                top = jnp.maximum(top, size_of[s : s + 8])
            peak[b] = jnp.maximum(peak[b], top)


def network_part(size, cols, history, delay, admittance, base, es, eg, wp, x, volt, vb):
    drive = jnp.zeros((size.scen, size.ends), F32)
    for d in range(size.delays):
        drive = jnp.where(delay == d + 1, history(d), drive)
    pair = stacked(drive)
    for b in range(size.blocks):
        added = folded(dot(pair, es[:, b * size.padded : (b + 1) * size.padded]))
        x[b] = stacked(base[b] + added)
    zeros = jnp.zeros((size.padded - size.width, 2 * size.padded), BF)

    def block_row(b, carry):
        left = jnp.concatenate([x[cols[k, b]] for k in range(size.picks)], axis=1)
        parts = []
        for k in range(size.picks):
            parts += [wp[b, k * size.width : (k + 1) * size.width, :], zeros]
        product = dot(left, jnp.concatenate(parts, axis=0))
        top, low = product[: size.scen], product[size.scen :]
        value = top[:, : size.padded] + top[:, size.padded :] + low[:, : size.padded]
        volt[b] = value
        vb[:, pl.ds(pl.multiple_of(b * size.padded, LANES), size.padded)] = stacked(value)
        return carry

    lax.fori_loop(0, size.blocks, block_row, 0, unroll=8)
    at_ends = folded(dot(vb[...], eg[...]))
    return 2.0 * admittance * at_ends - drive


def fault_terms(size, node, kind):
    first = lax.axis_index("region") * size.nodes
    local = (node[...] - first).astype(F32)
    inside = (local >= 0.0) & (local < size.nodes)
    site = jnp.where(inside, padded_index(local, size.width, size.padded), -1.0)
    level = 0.25 * jnp.left_shift(1, kind[...]).astype(F32)
    square = (size.scen, size.scen)
    diagonal = iota(square, 0) == iota(square, 1)

    def column(row):
        spread = jnp.where(diagonal, jnp.broadcast_to(row, square), 0.0)
        return jnp.broadcast_to(
            jnp.sum(spread, axis=1, keepdims=True), (size.scen, size.padded)
        )

    return column(site).astype(I32), column(level)


def turned_row(row):
    return jnp.broadcast_to(row, (LANES, row.shape[1])).T


def start_kernel(
    size,
    cols, received, inverse, source, decay, gain, voltage, branch_init, waves,
    line_node, delay, admittance, fault_node, fault_kind,
    wp, eg, es, cg, cs, prm, filt, amps, volt, vb, branch, node_rows, peak, fault_cols, up, down,
    raw, base, x, sems,
):
    stage = size.blocks // sems.shape[0]
    copies = []
    for i in range(sems.shape[0]):
        part = pl.ds(i * stage, stage)
        copies.append(pltpu.make_async_copy(inverse.at[part], raw.at[part], sems.at[i]))
        copies[-1].start()
    rows, capacity, slots = size.rows, size.capacity, size.slots
    regions, lanes = size.regions, size.lanes

    spare = size.slot_lanes - slots
    settings = [received[r * rows + capacity : r * rows + capacity + 4, :rows] for r in range(regions)]
    if spare:
        settings.append(jnp.zeros((4, spare), F32))
    prm[0:4, :] = jnp.concatenate(settings, axis=1)
    for c in range(0, size.slot_lanes, LANES):
        count = min(LANES, slots - c)
        within = lax.rem(iota((count, 2 * size.scen), 0) + c, rows)
        piece = jnp.where(within < capacity, received[c : c + count, :], 0.0)
        if count < LANES:
            piece = jnp.concatenate([piece, jnp.zeros((LANES - count, 2 * size.scen), F32)], axis=0)
        turned = piece.T
        filt[:, c : c + LANES] = turned[: size.scen]
        amps[:, c : c + LANES] = turned[size.scen :]

    def sites(row, gather, scatter):
        for c in range(0, row.shape[1], LANES):
            part = row[:, c : c + LANES]
            down_delta = part - iota((LANES, LANES), 0).astype(F32)
            across_delta = turned_row(part) - iota((LANES, LANES), 1).astype(F32)
            for n in range(0, lanes, LANES):
                gather[n : n + LANES, c : c + LANES] = one_hot(down_delta == float(n))
                scatter[c : c + LANES, n : n + LANES] = one_hot(across_delta == float(n))

    sites(padded_index(prm[3:4, :], size.width, size.padded), cg, cs)
    sites(padded_index(line_node[...].astype(F32), size.width, size.padded), eg, es)

    def put_voltage(b, value):
        volt[b] = value
        vb[:, b * size.padded : (b + 1) * size.padded] = stacked(value)

    def put_branch(b, value):
        branch[b] = value

    pad_blocks(size, voltage, put_voltage)
    pad_blocks(size, branch_init, put_branch)
    for i, vector in enumerate((source, decay, gain)):
        def put_row(b, value, i=i):
            node_rows[b, i : i + 1, :] = value

        pad_blocks(size, vector, put_row)
    site, level = fault_terms(size, fault_node, fault_kind)
    fault_cols[0] = site.astype(F32)
    fault_cols[1] = level
    converter_part(
        size, vb, cg, cs, prm, filt, amps, volt, branch, node_rows, None, (site, level), base
    )
    peak[...] = jnp.zeros(peak.shape, F32)

    for i, copy in enumerate(copies):
        copy.wait()

        def turn(b, carry):
            for k in range(size.picks):
                high, low = split_2(raw[b, k].T)
                zeros = jnp.zeros((size.width, size.padded - size.width), BF)
                wp[b, k * size.width : (k + 1) * size.width, :] = jnp.concatenate(
                    [high, zeros, low, zeros], axis=1
                )
            return carry

        lax.fori_loop(i * stage, (i + 1) * stage, turn, 0)

    launch = network_part(
        size, cols, lambda d: waves[d], delay[...], admittance[...], base, es, eg, wp, x, volt, vb
    )
    up[...] = launch[:, size.lines :]
    down[...] = launch[:, : size.lines]


def middle_kernel(size, last, vb, cg, cs, prm, volt, node_rows, fault_cols, *refs):
    refs = refs[4:]
    filt, amps, branch, peak, base = refs[:5]
    fault = (fault_cols[0].astype(I32), fault_cols[1])
    converter_part(size, vb, cg, cs, prm, filt, amps, volt, branch, node_rows, peak, fault, base)
    if last:
        back, branch_out = refs[5:]
        for c in range(0, size.slot_lanes, LANES):
            count = min(LANES, size.slots - c)
            part = jnp.concatenate([filt[:, c : c + LANES], amps[:, c : c + LANES]], axis=0)
            back[c : c + count, :] = part.T[:count]
        unpad_blocks(size, lambda b: branch[b], branch_out)


def step_kernel(size, last, done, cols, wp, eg, es, base, delay, admittance, waves, *refs):
    arrivals, refs = refs[: 2 * done], refs[2 * done :]

    def history(d):
        if d >= done:
            return waves[d - done]
        return jnp.concatenate([arrivals[2 * d][...], arrivals[2 * d + 1][...]], axis=1)

    if not last:
        volt, vb, up, down, x = refs
    else:
        peak, back, chunks, voltage_out, peak_out, volt, vb, x = refs
    launch = network_part(
        size, cols, history, delay[...], admittance[...], base, es, eg, wp, x, volt, vb
    )
    if not last:
        up[...] = launch[:, size.lines :]
        down[...] = launch[:, : size.lines]
        return
    rows = size.rows
    for r in range(size.regions):
        chunks[r, :rows, :] = back[r * rows : (r + 1) * rows, :]
    here = lax.axis_index("region")
    after = lax.rem(here + 1, size.regions)
    ahead = lax.rem(here + size.regions - 1, size.regions)
    chunks[after, rows : rows + size.scen, :] = launch[:, size.lines :]
    chunks[ahead, rows : rows + size.scen, :] = launch[:, : size.lines]
    unpad_blocks(size, lambda b: volt[b], voltage_out)

    def largest(b):
        top = jnp.max(jnp.abs(volt[b]), axis=0, keepdims=True)
        return jnp.maximum(top, jnp.max(peak[b], axis=0, keepdims=True))

    unpad_blocks(size, largest, peak_out)


def end_kernel(size, done, peaks, dst, received, waves, *refs):
    own, refs = refs[:peaks], refs[peaks:]
    arrivals, (state_out, waves_out, envelope_out) = refs[: 2 * done], refs[2 * done :]
    here = lax.axis_index("region")
    after = lax.rem(here + 1, size.regions)
    ahead = lax.rem(here + size.regions - 1, size.regions)
    rows, lines = size.rows, size.lines
    waves_out[0, :, :lines] = received[ahead, rows : rows + size.scen, :]
    waves_out[0, :, lines:] = received[after, rows : rows + size.scen, :]
    for d in range(1, size.delays):
        if d <= done:
            waves_out[d, :, :lines] = arrivals[2 * (d - 1)][...]
            waves_out[d, :, lines:] = arrivals[2 * (d - 1) + 1][...]
        else:
            waves_out[d] = waves[d - done - 1]
    top = own[0][...]
    for other in own[1:]:
        top = jnp.maximum(top, other[...])
    envelope_out[...] = top
    returned = jnp.concatenate([received[r, :rows, :] for r in range(size.regions)], axis=0)
    select = one_hot(iota((size.slots, size.convs), 0) == dst[...])
    parts = jnp.concatenate(split_3(returned.T), axis=0)
    state = dot(parts, select)
    width = 2 * size.scen
    state = state[:width] + state[width : 2 * width] + state[2 * width :]
    state_out[0] = state[: size.scen]
    state_out[1] = state[size.scen :]


def shape(dims, dtype=F32):
    return jax.ShapeDtypeStruct(dims, dtype)


def in_vmem(*values):
    return [pltpu.with_memory_space_constraint(v, pltpu.VMEM) for v in values]


def shards(
    inverse_blocks, block_cols, source_current, node_decay, node_gain, voltage_init, branch_init,
    wave_init, line_node, line_delay, line_admittance, conv_region, conv_node, conv_power,
    conv_gains, conv_init, fault_node, fault_kind,
):
    size = Sizes(inverse_blocks, voltage_init, wave_init, line_node, conv_node)
    regions, rows, scen = size.regions, size.rows, size.scen
    ring = [(i, (i + 1) % regions) for i in range(regions)]
    back_ring = [(j, i) for i, j in ring]

    def row(vector):
        return vector.reshape(1, -1)

    def call(kernel, name, outs, args, specs, scratch=(), aliases=None):
        return pl.pallas_call(
            kernel,
            name=name,
            out_shape=outs,
            in_specs=specs,
            out_specs=[VMEM] * len(outs),
            scratch_shapes=list(scratch),
            input_output_aliases=aliases or {},
            compiler_params=PARAMS,
        )(*args)

    packed, dst = call(
        functools.partial(pack_kernel, size),
        "pack",
        [shape((regions, rows, 2 * scen)), shape((1, size.convs), I32)],
        [row(conv_region), row(conv_node), row(conv_power), conv_gains, conv_init],
        [VMEM] * 5,
    )
    received = lax.all_to_all(packed, "region", split_axis=0, concat_axis=0, tiled=True)
    received = received.reshape(size.slots, 2 * scen)

    cols = block_cols.T
    delay, admittance = row(line_delay), row(line_admittance)
    state = (size.blocks, scen, size.padded)
    wide = (2 * scen, size.lanes)
    exchange = shape((scen, size.lines))
    x_scratch = pltpu.VMEM((size.blocks, 2 * scen, size.padded), BF)
    outs = [
        size.vmem((size.blocks, size.picks * size.width, 2 * size.padded), BF),
        size.vmem((size.lanes, size.ends), BF),
        size.vmem((size.ends, size.lanes), BF),
        size.vmem((size.lanes, size.slot_lanes), BF),
        size.vmem((size.slot_lanes, size.lanes), BF),
        size.vmem((8, size.slot_lanes)),
        size.vmem((scen, size.slot_lanes)),
        size.vmem((scen, size.slot_lanes)),
        size.vmem(state),
        size.vmem(wide, BF),
        size.vmem(state),
        size.vmem((size.blocks, 8, size.padded)),
        size.vmem((size.blocks, 8, size.padded)),
        size.vmem((2, scen, size.padded)),
        exchange,
        exchange,
    ]
    args = [
        cols, received, inverse_blocks, row(source_current), row(node_decay), row(node_gain),
        voltage_init, branch_init, wave_init, row(line_node), delay, admittance, row(fault_node),
        row(fault_kind),
    ]
    (
        wp, eg, es, cg, cs, prm, filt, amps, volt, vb, branch, node_rows, peak, fault_cols, up, down,
    ) = call(
        functools.partial(start_kernel, size),
        "start",
        outs,
        args,
        [SMEM, VMEM, HBM] + [VMEM] * 11,
        [
            pltpu.VMEM(inverse_blocks.shape, F32),
            pltpu.VMEM(state, F32),
            x_scratch,
            pltpu.SemaphoreType.DMA((4,)),
        ],
    )

    arrivals = []
    for step in range(1, STEPS):
        last = step == STEPS - 1
        from_ahead = lax.ppermute(up, "region", ring)
        from_after = lax.ppermute(down, "region", back_ring)
        outs = [
            size.vmem((scen, size.slot_lanes)),
            size.vmem((scen, size.slot_lanes)),
            size.vmem(state),
            size.vmem((size.blocks, 8, size.padded)),
            size.vmem(state),
        ]
        if last:
            outs += [size.vmem((size.slots, 2 * scen)), shape((scen, size.nodes))]
        result = call(
            functools.partial(middle_kernel, size, last),
            "middle",
            outs,
            in_vmem(vb, cg, cs, prm, volt, node_rows, fault_cols, filt, amps, branch, peak),
            [VMEM] * 11,
            aliases={7: 0, 8: 1, 9: 2, 10: 3},
        )
        filt, amps, branch, peak, base = result[:5]
        arrivals = [from_ahead, from_after] + arrivals
        args = [cols] + in_vmem(wp, eg, es, base) + [delay, admittance, wave_init] + arrivals
        specs = [SMEM] + [VMEM] * (len(args) - 1)
        if not last:
            volt, vb, up, down = call(
                functools.partial(step_kernel, size, False, step),
                "step",
                [size.vmem(state), size.vmem(wide, BF), exchange, exchange],
                args,
                specs,
                [x_scratch],
            )
            continue
        back, branch_out = result[5:]
        chunks, voltage_out, peak_out = call(
            functools.partial(step_kernel, size, True, step),
            "step",
            [
                shape((regions, rows + scen, 2 * scen)),
                shape((scen, size.nodes)),
                shape((1, size.nodes)),
            ],
            args + in_vmem(peak, back),
            specs + [VMEM] * 2,
            [pltpu.VMEM(state, F32), pltpu.VMEM(wide, BF), x_scratch],
        )

    others = lax.axis_size("scen")
    peaks = [peak_out] + [
        lax.ppermute(peak_out, "scen", [(i, (i + d) % others) for i in range(others)])
        for d in range(1, others)
    ]
    returned = lax.all_to_all(chunks, "region", split_axis=0, concat_axis=0, tiled=True)
    args = [dst, returned, wave_init] + peaks + arrivals
    conv_state, wave_history, envelope = call(
        functools.partial(end_kernel, size, STEPS - 1, len(peaks)),
        "end",
        [shape(conv_init.shape), shape(wave_init.shape), shape((1, size.nodes))],
        args,
        [VMEM] * len(args),
    )
    return voltage_out, branch_out, wave_history, conv_state, envelope.reshape(-1)


def solution(mesh):
    placed = (
        P("region", None, None, None),
        P("region", None),
        P("region"),
        P("region"),
        P("region"),
        P("scen", "region"),
        P("scen", "region"),
        P(None, "scen", "region"),
        P("region"),
        P("region"),
        P("region"),
        P("region", None),
        P("region"),
        P("region"),
        P(None, "region"),
        P(None, "scen", "region"),
        P("scen"),
        P("scen"),
    )
    return jax.shard_map(
        shards,
        mesh=mesh,
        in_specs=placed,
        out_specs=(
            P("scen", "region"),
            P("scen", "region"),
            P(None, "scen", "region"),
            P(None, "scen", "region"),
            P("region"),
        ),
        check_vma=False,
    )
```

profile of v0, /device:TPU:0, one launch (start us, length us, event | category | flops | bytes accessed | tf_op | source)
XLA Modules:
  0.0 131.5 jit_solution(11514375924363233951)
XLA Ops:
  2.0 0.9 copy-done.18
  4.3 1.2 pack.1
  5.4 20.9 %all_to_all.10 = f32[8,120,128]{2,1,0:T(8,128)S(1)} all-to-all(f32[8,120,128]{2,1,0:T(8,128)S(1)} %get-tuple-element.51), channel_id=1, replica_groups=mesh['region'=8,'scen'=4] {'region'}, dimensions={0} | all-to-all | bytes 983040 | tf_op jit(solution)/shard_map/all_to_all | solution.py:411
  26.4 1.0 copy-done.4
  27.4 1.1 copy-done.7
  28.5 1.1 copy-done.8
  35.8 21.0 %start.1 = (bf16[32,480,256]{2,1,0:T(8,128)(2,1)S(1)}, bf16[4096,256]{1,0:T(8,128)(2,1)S(1)}, bf16[256,4096]{1,0:T(8,128)(2,1)S(1)}, bf16[4096,1024]{1,0:T(8,128...) custom-call(s32[5,32]{1,0:T(8,128)S(1)} %bitcast.13, ...), custom_call_target="tpu_custom_call" | custom-call | tf_op jit(solution)/shard_map/start/pallas_call | solution.py:393
  56.9 1.5 %collective-permute-start = (f32[64,128]{1,0:T(8,128)S(1)}, f32[64,128]{1,0:T(8,128)S(1)}, u32[]{:S(2)}, u32[]{:S(2)}) collective-permute-start(f32[64,128]{1,0:T(8,128)S(1)} %get-tuple-element.67), channel_id=1, source_target_pairs={{0,4},{4,8},{8,12},{12,16},{16,20},{20,24},{24,28},{28,0},{1,5},{5... | collective-permute-start | bytes 98312 | tf_op jit(solution)/shard_map/ppermute | solution.py:462
  58.4 3.3 %collective-permute-start.1 = (f32[64,128]{1,0:T(8,128)S(1)}, f32[64,128]{1,0:T(8,128)S(1)}, u32[]{:S(2)}, u32[]{:S(2)}) collective-permute-start(f32[64,128]{1,0:T(8,128)S(1)} %get-tuple-element.68), channel_id=1, source_target_pairs={{4,0},{8,4},{12,8},{16,12},{20,16},{24,20},{28,24},{0,28},{5,1},{9... | collective-permute-start | bytes 98312 | tf_op jit(solution)/shard_map/ppermute | solution.py:463
  61.7 4.5 %middle.3 = (f32[64,1024]{1,0:T(8,128)S(1)}, f32[64,1024]{1,0:T(8,128)S(1)}, f32[32,64,128]{2,1,0:T(8,128)S(1)}, f32[32,8,128]{2,1,0:T(8,128)S(1)}, f32[32,64,128]{2,1,0:T(8,128)S(1)}) custom-call(bf16[128,4096]{1,0:T(8,128)(2,1)S(1)} %get-tuple-element.55.vb, ...), custom_call_target="tpu_custom_call", output_to_operand_aliasing={{0}: (7, {}), {1}: (8, {}), {2}: (9, {}), {3}: (10, {})} | custom-call | tf_op jit(solution)/shard_map/middle/pallas_call | solution.py:393
  66.3 3.2 %copy-done.1 = bf16[32,480,256]{2,1,0:T(8,128)(2,1)S(1)} copy-done((bf16[32,480,256]{2,1,0:T(8,128)(2,1)S(1)}, bf16[32,480,256]{2,1,0:T(8,128)(2,1)}, u32[]{:S(2)}) %copy-start.1) | copy-done | bytes 7864344
  69.5 1.6 %copy-done.3 = bf16[256,4096]{1,0:T(8,128)(2,1)S(1)} copy-done((bf16[256,4096]{1,0:T(8,128)(2,1)S(1)}, bf16[256,4096]{1,0:T(8,128)(2,1)}, u32[]{:S(2)}) %copy-start.3) | copy-done | bytes 2097176
  71.1 4.2 %step.3 = (f32[32,64,128]{2,1,0:T(8,128)S(1)}, bf16[128,4096]{1,0:T(8,128)(2,1)S(1)}, f32[64,128]{1,0:T(8,128)S(1)}, f32[64,128]{1,0:T(8,128)S(1)}) custom-call(s32[5,32]{1,0:T(8,128)S(1)} %bitcast.14, bf16[32,480,256]{2,1,0:T(8,128)(2,1)S(1)} %copy-done.1, bf16[4096,256]{1,0:T(8,128)(2,1)S(1)} %get-tuple-element.53.eg, bf16[256,4096]{1,0:T(8,128)(2,1)S(1)} %copy-done.3, ...), custom_call_target="tpu_custom_call" | custom-call | tf_op jit(solution)/shard_map/step/pallas_call | solution.py:393
  75.4 4.7 %collective-permute-start.3 = (f32[64,128]{1,0:T(8,128)S(1)}, f32[64,128]{1,0:T(8,128)S(1)}, u32[]{:S(2)}, u32[]{:S(2)}) collective-permute-start(f32[64,128]{1,0:T(8,128)S(1)} %get-tuple-element.77), channel_id=1, source_target_pairs={{4,0},{8,4},{12,8},{16,12},{20,16},{24,20},{28,24},{0,28},{5,1},{9... | collective-permute-start | bytes 98312 | tf_op jit(solution)/shard_map/ppermute | solution.py:463
  80.1 4.5 %middle.4 = (f32[64,1024]{1,0:T(8,128)S(1)}, f32[64,1024]{1,0:T(8,128)S(1)}, f32[32,64,128]{2,1,0:T(8,128)S(1)}, f32[32,8,128]{2,1,0:T(8,128)S(1)}, f32[32,64,128]{2,1,0:T(8,128)S(1)}) custom-call(bf16[128,4096]{1,0:T(8,128)(2,1)S(1)} %get-tuple-element.69.vb, ...), custom_call_target="tpu_custom_call", output_to_operand_aliasing={{0}: (7, {}), {1}: (8, {}), {2}: (9, {}), {3}: (10, {})} | custom-call | tf_op jit(solution)/shard_map/middle/pallas_call | solution.py:393
  84.7 4.2 %step.4 = (f32[32,64,128]{2,1,0:T(8,128)S(1)}, bf16[128,4096]{1,0:T(8,128)(2,1)S(1)}, f32[64,128]{1,0:T(8,128)S(1)}, f32[64,128]{1,0:T(8,128)S(1)}) custom-call(s32[5,32]{1,0:T(8,128)S(1)} %bitcast.15, bf16[32,480,256]{2,1,0:T(8,128)(2,1)S(1)} %copy-done.1, bf16[4096,256]{1,0:T(8,128)(2,1)S(1)} %get-tuple-element.53.eg, bf16[256,4096]{1,0:T(8,128)(2,1)S(1)} %copy-done.3, ...), custom_call_target="tpu_custom_call" | custom-call | tf_op jit(solution)/shard_map/step/pallas_call | solution.py:393
  89.0 4.7 %collective-permute-start.5 = (f32[64,128]{1,0:T(8,128)S(1)}, f32[64,128]{1,0:T(8,128)S(1)}, u32[]{:S(2)}, u32[]{:S(2)}) collective-permute-start(f32[64,128]{1,0:T(8,128)S(1)} %get-tuple-element.86), channel_id=1, source_target_pairs={{4,0},{8,4},{12,8},{16,12},{20,16},{24,20},{28,24},{0,28},{5,1},{9... | collective-permute-start | bytes 98312 | tf_op jit(solution)/shard_map/ppermute | solution.py:463
  93.7 5.3 %middle.5 = (f32[64,1024]{1,0:T(8,128)S(1)}, f32[64,1024]{1,0:T(8,128)S(1)}, f32[32,64,128]{2,1,0:T(8,128)S(1)}, f32[32,8,128]{2,1,0:T(8,128)S(1)}, f32[32,64,12...) custom-call(bf16[128,4096]{1,0:T(8,128)(2,1)S(1)} %get-tuple-element, ...), custom_call_target="tpu_custom_call", output_to_operand_aliasing={{0}: (7, {}), {1}: (8, {}), {2}: (9, {}), {3}: (10, {})} | custom-call | tf_op jit(solution)/shard_map/middle/pallas_call | solution.py:393
  99.1 5.1 %step.5 = (f32[8,184,128]{2,1,0:T(8,128)S(1)}, f32[64,3072]{1,0:T(8,128)}, f32[1,3072]{1,0:T(1,128)S(1)}) custom-call(s32[5,32]{1,0:T(8,128)S(1)} %bitcast.16, bf16[32,480,256]{2,1,0:T(8,128)(2,1)S(1)} %copy-done.1, bf16[4096,256]{1,0:T(8,128)(2,1)S(1)} %get-tuple-element.53.eg, bf16[256,4096]{1,0:T(8,128)(2,1)S(1)} %copy-done.3, ...), custom_call_target="tpu_custom_call" | custom-call | tf_op jit(solution)/shard_map/step/pallas_call | solution.py:393
  104.3 0.9 copy-done.9
  105.1 3.5 %all-to-all-start.1 = ((f32[8,184,128]{2,1,0:T(8,128)}), f32[8,184,128]{2,1,0:T(8,128)S(1)}, u32[]{:S(2)}, u32[]{:S(2)}) async-start(f32[8,184,128]{2,1,0:T(8,128)} %copy-done.9), calls=%async_computation.1 | async-start | bytes 1507328 | tf_op jit(solution)/shard_map/all_to_all | solution.py:514
  108.8 1.5 %collective-permute-start.7 = (f32[1,3072]{1,0:T(1,128)S(1)}, f32[1,3072]{1,0:T(1,128)S(1)}, u32[]{:S(2)}, u32[]{:S(2)}) collective-permute-start(f32[1,3072]{1,0:T(1,128)S(1)} %get-tuple-element.93.refs_0_), channel_id=1, source_target_pairs={{0,2},{1,3},{2,0},{3,1},{4,6},{5,7},{6,4},{7,5},{8,10},{9,11},{10,... | collective-permute-start | bytes 36872 | tf_op jit(solution)/shard_map/ppermute | solution.py:511
  110.5 2.0 %collective-permute-done.7.refs_2_ = f32[1,3072]{1,0:T(1,128)S(1)} collective-permute-done((f32[1,3072]{1,0:T(1,128)S(1)}, f32[1,3072]{1,0:T(1,128)S(1)}, u32[]{:S(2)}, u32[]{:S(2)}) %collective-permute-start.7) | collective-permute-done | bytes 12320 | tf_op jit(solution)/shard_map/ppermute | solution.py:511
  112.5 0.9 collective-permute-done.6.refs_1_
  113.4 12.2 %all-to-all-done.1.received = f32[8,184,128]{2,1,0:T(8,128)S(1)} async-done(((f32[8,184,128]{2,1,0:T(8,128)}), f32[8,184,128]{2,1,0:T(8,128)S(1)}, u32[]{:S(2)}, u32[]{:S(2)}) %all-to-all-start.1) | async-done | bytes 753696 | tf_op jit(solution)/shard_map/all_to_all | solution.py:514
  125.6 0.8 copy-done.11
  126.3 0.8 copy-done.13
  127.1 0.8 copy-done.15
  127.9 0.8 copy-done.17
  128.6 0.8 copy-done.20
  129.4 0.8 copy-done.22
  130.1 1.4 %end.1 = (f32[2,64,384]{2,1,0:T(8,128)}, f32[8,64,256]{2,1,0:T(8,128)}, f32[1,3072]{1,0:T(1,128)}) custom-call(s32[1,384]{1,0:T(1,128)S(1)} %get-tuple-element.91.dst, f32[8,184,128]{2,1,0:T(8,128)S(1)} %all-to-all-done.1.received, f32[8,64,256]{2,1,0:T(8,128)S(1)} %copy-done.6, f32[1,3072]{1,0:T(1,128)S(1)} %get-tuple-element.93.refs_0_, ...), custom_call_target="tpu_custom_call" | custom-call | tf_op jit(solution)/shard_map/end/pallas_call | solution.py:393
  (72 shorter events, 9.3 us)
Async XLA Ops:
  2.0 0.9 copy-start.18
  26.4 1.0 copy-start.4
  27.4 1.1 copy-start.7
  28.5 1.1 copy-start.8
  56.9 9.3 %copy-start = (bf16[32,480,256]{2,1,0:T(8,128)(2,1)}, bf16[32,480,256]{2,1,0:T(8,128)(2,1)S(1)}, u32[]{:S(2)}) copy-start(bf16[32,480,256]{2,1,0:T(8,128)(2,1)S(1)} %get-tuple-element.52.wp) | copy-start | bytes 23592964
  56.9 9.3 %copy-start.2 = (bf16[256,4096]{1,0:T(8,128)(2,1)}, bf16[256,4096]{1,0:T(8,128)(2,1)S(1)}, u32[]{:S(2)}) copy-start(bf16[256,4096]{1,0:T(8,128)(2,1)S(1)} %get-tuple-element.54.es) | copy-start | bytes 6291460
  56.9 9.3 %collective-permute-start = (f32[64,128]{1,0:T(8,128)S(1)}, f32[64,128]{1,0:T(8,128)S(1)}, u32[]{:S(2)}, u32[]{:S(2)}) collective-permute-start(f32[64,128]{1,0:T(8,128)S(1)} %get-tuple-element.67), channel_id=1, source_target_pairs={{0,4},{4,8},{8,12},{12,16},{16,20},{20,24},{24,28},{28,0},{1,5},{5... | collective-permute-start | bytes 98312 | tf_op jit(solution)/shard_map/ppermute | solution.py:462
  58.4 7.8 %collective-permute-start.1 = (f32[64,128]{1,0:T(8,128)S(1)}, f32[64,128]{1,0:T(8,128)S(1)}, u32[]{:S(2)}, u32[]{:S(2)}) collective-permute-start(f32[64,128]{1,0:T(8,128)S(1)} %get-tuple-element.68), channel_id=1, source_target_pairs={{4,0},{8,4},{12,8},{16,12},{20,16},{24,20},{28,24},{0,28},{5,1},{9... | collective-permute-start | bytes 98312 | tf_op jit(solution)/shard_map/ppermute | solution.py:463
  61.7 4.6 %copy-start.5 = (f32[8,64,256]{2,1,0:T(8,128)S(1)}, f32[8,64,256]{2,1,0:T(8,128)}, u32[]{:S(2)}) copy-start(f32[8,64,256]{2,1,0:T(8,128)} %waves.9) | copy-start | bytes 1572868
  61.7 4.6 %copy-start.25 = (s32[256]{0:T(256)S(1)}, s32[256]{0:T(256)}, u32[]{:S(2)}) copy-start(s32[256]{0:T(256)} %param.27) | copy-start | bytes 3076
  61.7 4.6 %copy-start.27 = (f32[256]{0:T(256)S(1)}, f32[256]{0:T(256)}, u32[]{:S(2)}) copy-start(f32[256]{0:T(256)} %param.28) | copy-start | bytes 3076
  66.2 32.8 %copy-start.10 = (f32[64,128]{1,0:T(8,128)}, f32[64,128]{1,0:T(8,128)S(1)}, u32[]{:S(2)}) copy-start(f32[64,128]{1,0:T(8,128)S(1)} %collective-permute-done.refs_0_.refs_2_.refs_4_.refs_8_) | copy-start | bytes 98308
  66.2 32.8 %copy-start.12 = (f32[64,128]{1,0:T(8,128)}, f32[64,128]{1,0:T(8,128)S(1)}, u32[]{:S(2)}) copy-start(f32[64,128]{1,0:T(8,128)S(1)} %collective-permute-done.1.refs_1_.refs_3_.refs_5_.refs_9_) | copy-start | bytes 98308
  66.3 3.2 %copy-start.1 = (bf16[32,480,256]{2,1,0:T(8,128)(2,1)S(1)}, bf16[32,480,256]{2,1,0:T(8,128)(2,1)}, u32[]{:S(2)}) copy-start(bf16[32,480,256]{2,1,0:T(8,128)(2,1)} %copy-done) | copy-start | bytes 23592964
  69.5 1.6 %copy-start.3 = (bf16[256,4096]{1,0:T(8,128)(2,1)S(1)}, bf16[256,4096]{1,0:T(8,128)(2,1)}, u32[]{:S(2)}) copy-start(bf16[256,4096]{1,0:T(8,128)(2,1)} %copy-done.2) | copy-start | bytes 6291460
  75.3 9.3 %collective-permute-start.2 = (f32[64,128]{1,0:T(8,128)S(1)}, f32[64,128]{1,0:T(8,128)S(1)}, u32[]{:S(2)}, u32[]{:S(2)}) collective-permute-start(f32[64,128]{1,0:T(8,128)S(1)} %get-tuple-element.76), channel_id=1, source_target_pairs={{0,4},{4,8},{8,12},{12,16},{16,20},{20,24},{24,28},{28,0},{1,5},{5... | collective-permute-start | bytes 98312 | tf_op jit(solution)/shard_map/ppermute | solution.py:462
  75.4 9.3 %collective-permute-start.3 = (f32[64,128]{1,0:T(8,128)S(1)}, f32[64,128]{1,0:T(8,128)S(1)}, u32[]{:S(2)}, u32[]{:S(2)}) collective-permute-start(f32[64,128]{1,0:T(8,128)S(1)} %get-tuple-element.77), channel_id=1, source_target_pairs={{4,0},{8,4},{12,8},{16,12},{20,16},{24,20},{28,24},{0,28},{5,1},{9... | collective-permute-start | bytes 98312 | tf_op jit(solution)/shard_map/ppermute | solution.py:463
  84.7 14.4 %copy-start.14 = (f32[64,128]{1,0:T(8,128)}, f32[64,128]{1,0:T(8,128)S(1)}, u32[]{:S(2)}) copy-start(f32[64,128]{1,0:T(8,128)S(1)} %collective-permute-done.2.refs_0_.refs_2_.refs_6_) | copy-start | bytes 98308
  84.7 14.4 %copy-start.16 = (f32[64,128]{1,0:T(8,128)}, f32[64,128]{1,0:T(8,128)S(1)}, u32[]{:S(2)}) copy-start(f32[64,128]{1,0:T(8,128)S(1)} %collective-permute-done.3.refs_1_.refs_3_.refs_7_) | copy-start | bytes 98308
  88.9 10.1 %collective-permute-start.4 = (f32[64,128]{1,0:T(8,128)S(1)}, f32[64,128]{1,0:T(8,128)S(1)}, u32[]{:S(2)}, u32[]{:S(2)}) collective-permute-start(f32[64,128]{1,0:T(8,128)S(1)} %get-tuple-element.85), channel_id=1, source_target_pairs={{0,4},{4,8},{8,12},{12,16},{16,20},{20,24},{24,28},{28,0},{1,5},{5... | collective-permute-start | bytes 98312 | tf_op jit(solution)/shard_map/ppermute | solution.py:462
  89.0 10.0 %collective-permute-start.5 = (f32[64,128]{1,0:T(8,128)S(1)}, f32[64,128]{1,0:T(8,128)S(1)}, u32[]{:S(2)}, u32[]{:S(2)}) collective-permute-start(f32[64,128]{1,0:T(8,128)S(1)} %get-tuple-element.86), channel_id=1, source_target_pairs={{4,0},{8,4},{12,8},{16,12},{20,16},{24,20},{28,24},{0,28},{5,1},{9... | collective-permute-start | bytes 98312 | tf_op jit(solution)/shard_map/ppermute | solution.py:463
  99.0 5.2 %copy-start.19 = (f32[64,128]{1,0:T(8,128)}, f32[64,128]{1,0:T(8,128)S(1)}, u32[]{:S(2)}) copy-start(f32[64,128]{1,0:T(8,128)S(1)} %collective-permute-done.4.refs_0_.refs_4_) | copy-start | bytes 98308
  99.0 5.2 %copy-start.21 = (f32[64,128]{1,0:T(8,128)}, f32[64,128]{1,0:T(8,128)S(1)}, u32[]{:S(2)}) copy-start(f32[64,128]{1,0:T(8,128)S(1)} %collective-permute-done.5.refs_1_.refs_5_) | copy-start | bytes 98308
  99.1 26.5 %copy-start.6 = (f32[8,64,256]{2,1,0:T(8,128)S(1)}, f32[8,64,256]{2,1,0:T(8,128)}, u32[]{:S(2)}) copy-start(f32[8,64,256]{2,1,0:T(8,128)} %waves.9) | copy-start | bytes 1572868
  104.2 0.9 copy-start.9
  105.1 20.4 %all-to-all-start.1 = ((f32[8,184,128]{2,1,0:T(8,128)}), f32[8,184,128]{2,1,0:T(8,128)S(1)}, u32[]{:S(2)}, u32[]{:S(2)}) async-start(f32[8,184,128]{2,1,0:T(8,128)} %copy-done.9), calls=%async_computation.1 | async-start | bytes 1507328 | tf_op jit(solution)/shard_map/all_to_all | solution.py:514
  108.7 1.8 %collective-permute-start.8 = (f32[1,3072]{1,0:T(1,128)S(1)}, f32[1,3072]{1,0:T(1,128)S(1)}, u32[]{:S(2)}, u32[]{:S(2)}) collective-permute-start(f32[1,3072]{1,0:T(1,128)S(1)} %get-tuple-element.93.refs_0_), channel_id=1, source_target_pairs={{0,3},{1,0},{2,1},{3,2},{4,7},{5,4},{6,5},{7,6},{8,11},{9,8},{10,9... | collective-permute-start | bytes 36872 | tf_op jit(solution)/shard_map/ppermute | solution.py:511
  108.8 3.8 %collective-permute-start.7 = (f32[1,3072]{1,0:T(1,128)S(1)}, f32[1,3072]{1,0:T(1,128)S(1)}, u32[]{:S(2)}, u32[]{:S(2)}) collective-permute-start(f32[1,3072]{1,0:T(1,128)S(1)} %get-tuple-element.93.refs_0_), channel_id=1, source_target_pairs={{0,2},{1,3},{2,0},{3,1},{4,6},{5,7},{6,4},{7,5},{8,10},{9,11},{10,... | collective-permute-start | bytes 36872 | tf_op jit(solution)/shard_map/ppermute | solution.py:511
  110.3 3.1 %collective-permute-start.6 = (f32[1,3072]{1,0:T(1,128)S(1)}, f32[1,3072]{1,0:T(1,128)S(1)}, u32[]{:S(2)}, u32[]{:S(2)}) collective-permute-start(f32[1,3072]{1,0:T(1,128)S(1)} %get-tuple-element.93.refs_0_), channel_id=1, source_target_pairs={{0,1},{1,2},{2,3},{3,0},{4,5},{5,6},{6,7},{7,4},{8,9},{9,10},{10,1... | collective-permute-start | bytes 36872 | tf_op jit(solution)/shard_map/ppermute | solution.py:511
  125.6 0.8 copy-start.11
  126.3 0.8 copy-start.13
  127.1 0.8 copy-start.15
  (14 other events, 9.8 us)
where the time goes:
time: 133 us; the launch traced here: 132 us
  Pallas kernels  51.5 us (39%)
  local copies, waits for them, and re-layouts  23.4 us (18%)
  blocking collectives  20.9 us (16%)
  starting transfers between devices  19.6 us (15%)
  waiting for transfers between devices  15.1 us (11%)
    pallas_call x9, Pallas kernels, call(): pl.pallas_call(kernel, name=name, out_shape=outs, in_specs=specs, out_spe...  51.5 us
    unnamed x72, local copies, waits for them, and re-layouts  22 us
    all_to_all x1, blocking collectives, shards(): lax.all_to_all(packed, 'region', split_axis=0, concat_axis=0, tiled=True)  20.9 us
    ppermute x3, starting transfers between devices, shards(): from_after = lax.ppermute(down, 'region', back_ring)  12.7 us
    all_to_all x1, waiting for transfers between devices, shards(): lax.all_to_all(chunks, 'region', split_axis=0, concat_axis=0, tiled=True)  12.2 us
    all_to_all x1, starting transfers between devices, shards(): lax.all_to_all(chunks, 'region', split_axis=0, concat_axis=0, tiled=True)  3.54 us
    ppermute x3, waiting for transfers between devices, shards(): lax.ppermute(peak_out, 'scen', [(i, (i + d) % others) for i in range(othe...  2.95 us
  transfers between devices with their start and end apart: 10, of which 3 were waited for; matrix products, arithmetic and copies ran while one was open for 0% of the time, Pallas kernels for 11%

commit v1 on v0

v1 whole, which is shorter than its diff:
```python
import functools
import math

import jax
import jax.numpy as jnp
from jax import lax
from jax.experimental import pallas as pl
from jax.experimental.pallas import tpu as pltpu
from jax.sharding import PartitionSpec as P

STEPS = 4
LANES = 128
BF = jnp.bfloat16
F32 = jnp.float32
I32 = jnp.int32
VMEM = pl.BlockSpec(memory_space=pltpu.VMEM)
SMEM = pl.BlockSpec(memory_space=pltpu.SMEM)
HBM = pl.BlockSpec(memory_space=pltpu.HBM)


def round_up(value, unit):
    return -(-value // unit) * unit


def iota(shape, dim):
    return lax.broadcasted_iota(I32, shape, dim)


def split_2(value):
    high = value.astype(BF)
    return high, (value - high.astype(F32)).astype(BF)


def split_3(value):
    high = value.astype(BF)
    rest = value - high.astype(F32)
    middle = rest.astype(BF)
    return high, middle, (rest - middle.astype(F32)).astype(BF)


def stacked(value):
    high, low = split_2(value)
    return jnp.concatenate([high, low], axis=0)


def folded(value):
    half = value.shape[0] // 2
    return value[:half] + value[half:]


def dot(left, right):
    return jnp.dot(left, right, preferred_element_type=F32)


def one_hot(mask):
    return jnp.where(mask, 1.0, 0.0).astype(BF)


def padded_index(nodes, width, padded):
    block = jnp.floor((nodes + 0.5) * (1.0 / width))
    return nodes + block * (padded - width)


class Sizes:
    def __init__(self, inverse_blocks, voltage, wave_init, line_node, conv_node):
        self.blocks, self.picks, self.width, _ = inverse_blocks.shape
        self.scen, self.nodes = voltage.shape
        self.delays = wave_init.shape[0]
        self.ends = line_node.shape[0]
        self.lines = self.ends // 2
        self.convs = conv_node.shape[0]
        self.regions = lax.axis_size("region")
        self.capacity = max(2, 12 * self.convs // (5 * self.regions))
        self.rows = round_up(self.capacity + 4, 8)
        self.slots = self.regions * self.rows
        self.slot_lanes = round_up(self.slots, LANES)
        self.padded = round_up(self.width, LANES)
        self.lanes = self.blocks * self.padded
        self.group = math.lcm(self.width, LANES) // self.width

        self.state = (self.blocks, self.scen, self.padded)
        self.wide = (2 * self.scen, self.lanes)
        self.weights = (self.blocks, self.picks * self.width, 2 * self.padded)
        self.site_rows = (self.lanes, self.ends)
        self.response = (self.blocks, self.ends, 2 * self.padded)
        self.coupling = (self.ends, 2 * self.ends)
        self.node_rows = (self.blocks, 8, self.padded)
        self.fault_cols = (2, self.scen, self.padded)
        self.drive = (self.scen, self.ends)
        self.exchange = (self.scen, self.lines)


class Copies:
    def __init__(self, sems):
        self.sems = sems
        self.count = 0

    def start(self, source, target):
        copy = pltpu.make_async_copy(source, target, self.sems.at[self.count])
        self.count += 1
        copy.start()
        return copy


def pad_blocks(size, source, store):
    group_width = size.group * size.width
    for first in range(0, size.blocks, size.group):
        chunk = source[:, first * size.width : first * size.width + group_width]
        for j in range(size.group):
            part = chunk[:, j * size.width : (j + 1) * size.width]
            zeros = jnp.zeros((part.shape[0], size.padded - size.width), part.dtype)
            store(first + j, jnp.concatenate([part, zeros], axis=1))


def unpad_blocks(size, load, target):
    group_width = size.group * size.width
    for first in range(0, size.blocks, size.group):
        parts = [load(first + j)[:, : size.width] for j in range(size.group)]
        target[:, first * size.width : first * size.width + group_width] = jnp.concatenate(
            parts, axis=1
        )


def block_lanes(size, b):
    return slice(b * size.padded, (b + 1) * size.padded)


def pack_kernel(size, table_hbm, init_hbm, out, dst_out, table, init, sems):
    convs, slots = size.convs, size.slots
    copies = Copies(sems)
    first = copies.start(table_hbm, table)
    second = copies.start(init_hbm, init)
    first.wait()
    target = table[0:1, :].astype(I32)
    member = iota((round_up(size.regions, 16), convs), 0) == target
    before = one_hot(iota((convs, convs), 0) < iota((convs, convs), 1))
    earlier = dot(one_hot(member), before)
    rank = jnp.sum(jnp.where(member, earlier, 0.0), axis=0, keepdims=True)
    dst = target * size.rows + rank.astype(I32)
    dst_out[...] = dst
    select = one_hot(iota((slots, convs), 0) == dst)
    settings = jnp.concatenate([table[1:5, :], jnp.zeros((LANES - 4, convs), F32)], axis=0)
    second.wait()
    state = jnp.concatenate([init[0], init[1]], axis=0)
    payload = jnp.concatenate([state.T, settings.T], axis=1)
    width = state.shape[0]
    rows = sum(dot(select, part) for part in split_3(payload))
    for r in range(size.regions):
        chunk = rows[r * size.rows : (r + 1) * size.rows]
        out[r] = chunk[:, :width]
        filler = jnp.zeros((LANES - size.rows, LANES), F32)
        turned = jnp.concatenate([chunk[:, width:], filler], axis=0).T
        out[r, size.capacity : size.capacity + 4, :] = turned[:4]


def fault_terms(size, node, kind):
    first = lax.axis_index("region") * size.nodes
    local = (node[...] - first).astype(F32)
    inside = (local >= 0.0) & (local < size.nodes)
    site = jnp.where(inside, padded_index(local, size.width, size.padded), -1.0)
    level = 0.25 * jnp.left_shift(1, kind[...]).astype(F32)
    square = (size.scen, size.scen)
    diagonal = iota(square, 0) == iota(square, 1)

    def column(row):
        spread = jnp.where(diagonal, jnp.broadcast_to(row, square), 0.0)
        return jnp.broadcast_to(jnp.sum(spread, axis=1, keepdims=True), (size.scen, size.padded))

    return column(site), column(level)


def turned_row(row):
    return jnp.broadcast_to(row, (LANES, row.shape[1])).T


def picked_product(size, cols, b, x, wp):
    zeros = jnp.zeros((size.padded - size.width, 2 * size.padded), BF)
    left = jnp.concatenate([x[cols[k, b]] for k in range(size.picks)], axis=1)
    parts = []
    for k in range(size.picks):
        parts += [wp[b, k * size.width : (k + 1) * size.width, :], zeros]
    return dot(left, jnp.concatenate(parts, axis=0))


def three_terms(product, rows, width):
    top, low = product[:rows], product[rows:]
    return top[:, :width] + top[:, width:] + low[:, :width]


def apply_inverse(size, cols, x, wp, volt, vb):
    def block_row(b, carry):
        value = three_terms(picked_product(size, cols, b, x, wp), size.scen, size.padded)
        volt[b] = value
        vb[:, pl.ds(pl.multiple_of(b * size.padded, LANES), size.padded)] = stacked(value)
        return carry

    lax.fori_loop(0, size.blocks, block_row, 0, unroll=8)


def prep_kernel(
    size,
    cols_hbm, inverse, source, decay, gain, voltage, branch_init, line_node, fault_node, fault_kind,
    wp_out, eg_out, mt_out, kk_out, vb_out, branch_out, rest_out, rows_out, fault_out,
    cols, raw, vectors, volt_in, branch_in, nodes, faults,
    wp, eg, es, mt, both, kk, vb, volt, branch, rest, node_rows, fault_cols,
    sems,
):
    copies = Copies(sems)
    cols_copy = copies.start(cols_hbm, cols)
    small = [
        copies.start(line_node, nodes),
        copies.start(fault_node, faults.at[0:1]),
        copies.start(fault_kind, faults.at[1:2]),
    ]
    small += [copies.start(v, vectors.at[i]) for i, v in enumerate((source, decay, gain))]
    large = [copies.start(voltage, volt_in), copies.start(branch_init, branch_in)]
    stages = 4
    stage = size.blocks // stages
    weight_copies = []
    for i in range(stages):
        part = pl.ds(i * stage, stage)
        weight_copies.append(copies.start(inverse.at[part], raw.at[part]))
    sent = []
    for copy in small:
        copy.wait()

    row = padded_index(nodes[...].astype(F32), size.width, size.padded)
    for c in range(0, size.ends, LANES):
        part = row[:, c : c + LANES]
        down_delta = part - iota((LANES, LANES), 0).astype(F32)
        across_delta = turned_row(part) - iota((LANES, LANES), 1).astype(F32)
        for n in range(0, size.lanes, LANES):
            eg[n : n + LANES, c : c + LANES] = one_hot(down_delta == float(n))
            b, lane = n // size.padded, n % size.padded
            es[b, c : c + LANES, lane : lane + LANES] = one_hot(across_delta == float(n))
    sent.append(copies.start(eg, eg_out))

    for i in range(3):
        def put_row(b, value, i=i):
            node_rows[b, i : i + 1, :] = value

        pad_blocks(size, vectors.at[i], put_row)
    sent.append(copies.start(node_rows, rows_out))
    site, level = fault_terms(size, faults.at[0:1], faults.at[1:2])
    fault_cols[0] = site
    fault_cols[1] = level
    sent.append(copies.start(fault_cols, fault_out))
    for copy in large:
        copy.wait()

    def put_voltage(b, value):
        volt[b] = value
        vb[:, block_lanes(size, b)] = stacked(value)

    def put_branch(b, value):
        history = node_rows[b, 1:2, :] * value + node_rows[b, 2:3, :] * volt[b]
        branch[b] = history
        rest[b] = rest_of(size, node_rows, b, history, volt[b], site, level)

    pad_blocks(size, volt_in, put_voltage)
    pad_blocks(size, branch_in, put_branch)
    sent.append(copies.start(vb, vb_out))
    sent.append(copies.start(branch, branch_out))
    sent.append(copies.start(rest, rest_out))

    cols_copy.wait()
    for i, copy in enumerate(weight_copies):
        copy.wait()

        def turn(b, carry):
            for k in range(size.picks):
                high, low = split_2(raw[b, k].T)
                zeros = jnp.zeros((size.width, size.padded - size.width), BF)
                wp[b, k * size.width : (k + 1) * size.width, :] = jnp.concatenate(
                    [high, zeros, low, zeros], axis=1
                )
            return carry

        lax.fori_loop(i * stage, (i + 1) * stage, turn, 0, unroll=2)
        part = pl.ds(i * stage, stage)
        sent.append(copies.start(wp.at[part], wp_out.at[part]))

    def respond(b, carry):
        product = picked_product(size, cols, b, es, wp)
        high, low = split_2(product[:, : size.padded] + product[:, size.padded :])
        mt[b] = jnp.concatenate([high, low], axis=1)
        both[:, pl.ds(pl.multiple_of(b * size.padded, LANES), size.padded)] = jnp.concatenate(
            [high, low], axis=0
        )
        return carry

    lax.fori_loop(0, size.blocks, respond, 0, unroll=4)
    sent.append(copies.start(mt, mt_out))
    high, low = split_2(folded(dot(both[...], eg[...])))
    kk[...] = jnp.concatenate([high, low], axis=1)
    sent.append(copies.start(kk, kk_out))
    for copy in sent:
        copy.wait()


def rest_of(size, node_rows, b, history, v, site, level):
    lane = iota((size.scen, size.padded), 1).astype(F32)
    hit = jnp.where(lane + float(b * size.padded) == site, level, 0.0)
    return node_rows[b, 0:1, :] - history - hit * v


def converter_update(size, vb, cg, prm, filt, amps):
    measured = folded(dot(vb[...], cg[...]))
    filtered = filt[...]
    filtered = filtered + prm[2:3, :] * (measured - filtered)
    current = amps[...]
    target = prm[0:1, :] * filtered / (1.0 + filtered * filtered)
    current = current + prm[1:2, :] * (target - current)
    filt[...] = filtered
    amps[...] = current
    return stacked(current)


def launch_part(size, history, ends, at_ends, kk, drive_out, up, down):
    drive = jnp.zeros(size.drive, F32)
    for d in range(size.delays):
        drive = jnp.where(ends[0:1, :] == float(d + 1), history(d), drive)
    drive_out[...] = drive
    answer = three_terms(dot(stacked(drive), kk[...]), size.scen, size.ends)
    launch = 2.0 * ends[1:2, :] * (at_ends + answer) - drive
    up[...] = launch[:, size.lines :]
    down[...] = launch[:, : size.lines]


def start_kernel(
    size,
    cols_hbm, received_hbm, waves_hbm, delay_hbm, admittance_hbm,
    wp_hbm, eg_hbm, mt_hbm, kk_hbm, vb_hbm, branch_hbm, rest_hbm, rows_hbm, fault_hbm,
    wp, eg, mt, kk, waves, ends, node_rows, fault_cols, branch, cg, cs, prm, filt, amps, volt,
    peak, drive, up, down,
    cols, received, line_rows, rest, x, vb, sems,
):
    copies = Copies(sems)
    received_copy = copies.start(received_hbm, received)
    vb_copy = copies.start(vb_hbm, vb)
    rest_copy = copies.start(rest_hbm, rest)
    cols_copy = copies.start(cols_hbm, cols)
    wp_copy = copies.start(wp_hbm, wp)
    later = [
        copies.start(eg_hbm, eg),
        copies.start(delay_hbm, line_rows.at[0]),
        copies.start(admittance_hbm, line_rows.at[1]),
        copies.start(waves_hbm, waves),
        copies.start(kk_hbm, kk),
        copies.start(mt_hbm, mt),
        copies.start(branch_hbm, branch),
        copies.start(rows_hbm, node_rows),
        copies.start(fault_hbm, fault_cols),
    ]
    rows, capacity, slots, regions = size.rows, size.capacity, size.slots, size.regions
    received_copy.wait()
    settings = [
        received[r * rows + capacity : r * rows + capacity + 4, :rows] for r in range(regions)
    ]
    spare = size.slot_lanes - slots
    if spare:
        settings.append(jnp.zeros((4, spare), F32))
    prm[0:4, :] = jnp.concatenate(settings, axis=1)
    for c in range(0, size.slot_lanes, LANES):
        count = min(LANES, slots - c)
        within = lax.rem(iota((count, 2 * size.scen), 0) + c, rows)
        piece = jnp.where(within < capacity, received[c : c + count, :], 0.0)
        if count < LANES:
            piece = jnp.concatenate([piece, jnp.zeros((LANES - count, 2 * size.scen), F32)], axis=0)
        turned = piece.T
        filt[:, c : c + LANES] = turned[: size.scen]
        amps[:, c : c + LANES] = turned[size.scen :]
    row = padded_index(prm[3:4, :], size.width, size.padded)
    for c in range(0, size.slot_lanes, LANES):
        part = row[:, c : c + LANES]
        down_delta = part - iota((LANES, LANES), 0).astype(F32)
        across_delta = turned_row(part) - iota((LANES, LANES), 1).astype(F32)
        for n in range(0, size.lanes, LANES):
            cg[n : n + LANES, c : c + LANES] = one_hot(down_delta == float(n))
            cs[c : c + LANES, n : n + LANES] = one_hot(across_delta == float(n))
    peak[...] = jnp.zeros(peak.shape, F32)

    vb_copy.wait()
    pair = converter_update(size, vb, cg, prm, filt, amps)
    rest_copy.wait()
    for b in range(size.blocks):
        injected = folded(dot(pair, cs[:, block_lanes(size, b)]))
        x[b] = stacked(rest[b] + injected)
    cols_copy.wait()
    wp_copy.wait()
    apply_inverse(size, cols, x, wp, volt, vb)
    for copy in later:
        copy.wait()
    ends[0:1, :] = line_rows[0].astype(F32)
    ends[1:2, :] = line_rows[1]
    at_ends = folded(dot(vb[...], eg[...]))
    launch_part(size, lambda d: waves[d], ends, at_ends, kk, drive, up, down)


def middle_kernel(
    size, last,
    cols_hbm, drive, wp, eg, mt, node_rows, fault_cols, cg, cs, prm,
    branch_in, filt_in, amps_in, volt_in, peak_in,
    branch, filt, amps, volt, peak, at_ends, *refs,
):
    if last:
        back, branch_out = refs[:2]
    cols, x, vb, sem = refs[-4:]
    cols_copy = pltpu.make_async_copy(cols_hbm, cols, sem)
    cols_copy.start()
    pair = stacked(drive[...])
    for b in range(size.blocks):
        added = three_terms(dot(pair, mt[b]), size.scen, size.padded)
        v = volt[b] + added
        volt[b] = v
        vb[:, block_lanes(size, b)] = stacked(v)
        magnitude = jnp.abs(v)
        top = magnitude[:8]
        for s in range(8, size.scen, 8):
            top = jnp.maximum(top, magnitude[s : s + 8])
        peak[b] = jnp.maximum(peak[b], top)
    pair = converter_update(size, vb, cg, prm, filt, amps)
    site, level = fault_cols[0], fault_cols[1]
    for b in range(size.blocks):
        injected = folded(dot(pair, cs[:, block_lanes(size, b)]))
        history = node_rows[b, 1:2, :] * branch[b] + node_rows[b, 2:3, :] * volt[b]
        branch[b] = history
        x[b] = stacked(rest_of(size, node_rows, b, history, volt[b], site, level) + injected)
    cols_copy.wait()
    apply_inverse(size, cols, x, wp, volt, vb)
    at_ends[...] = folded(dot(vb[...], eg[...]))
    if last:
        for c in range(0, size.slot_lanes, LANES):
            count = min(LANES, size.slots - c)
            part = jnp.concatenate([filt[:, c : c + LANES], amps[:, c : c + LANES]], axis=0)
            back[c : c + count, :] = part.T[:count]
        unpad_blocks(size, lambda b: branch[b], branch_out)


def launch_kernel(size, done, last, at_ends, kk, ends, waves, *refs):
    arrivals, refs = refs[: 2 * done], refs[2 * done :]

    def history(d):
        if d >= done:
            return waves[d - done]
        return jnp.concatenate([arrivals[2 * d][...], arrivals[2 * d + 1][...]], axis=1)

    if last:
        back, refs = refs[0], refs[1:]
    drive, up, down = refs[:3]
    if last:
        chunks, waves_out, recent, sems = refs[3:]
        copies = Copies(sems)
        sent = [copies.start(back, chunks)]
        for d in range(done):
            recent[d] = history(d)
        sent.append(copies.start(recent, waves_out.at[pl.ds(1, done)]))
        kept = size.delays - 1 - done
        sent.append(copies.start(waves.at[pl.ds(0, kept)], waves_out.at[pl.ds(1 + done, kept)]))
    launch_part(size, history, ends, at_ends[...], kk, drive, up, down)
    if last:
        for copy in sent:
            copy.wait()


def final_kernel(size, drive, volt_hbm, mt_hbm, peak_hbm, voltage_out, peak_out, volt, mt, peak, sems):
    copies = Copies(sems)
    half = size.blocks // 2
    parts = []
    for i in range(2):
        part = pl.ds(i * half, half)
        parts.append(
            [copies.start(volt_hbm.at[part], volt.at[part]), copies.start(mt_hbm.at[part], mt.at[part])]
        )
    peak_copy = copies.start(peak_hbm, peak)
    pair = stacked(drive[...])
    for b in range(size.blocks):
        if b % half == 0:
            for copy in parts[b // half]:
                copy.wait()
        volt[b] = volt[b] + three_terms(dot(pair, mt[b]), size.scen, size.padded)
    unpad_blocks(size, lambda b: volt[b], voltage_out)
    peak_copy.wait()

    def largest(b):
        top = jnp.max(jnp.abs(volt[b]), axis=0, keepdims=True)
        return jnp.maximum(top, jnp.max(peak[b], axis=0, keepdims=True))

    unpad_blocks(size, largest, peak_out)


def end_kernel(size, peaks, dst_hbm, received_hbm, ahead, after, waves_in, *refs):
    own, refs = refs[:peaks], refs[peaks:]
    state_out, waves_out, envelope_out, dst, received, newest, tops, sems = refs
    copies = Copies(sems)
    received_copy = copies.start(received_hbm, received)
    dst_copy = copies.start(dst_hbm, dst)
    top_copies = [copies.start(ref, tops.at[i]) for i, ref in enumerate(own)]
    lines = size.lines
    newest[0, :, :lines] = ahead[...]
    newest[0, :, lines:] = after[...]
    newest_copy = copies.start(newest, waves_out.at[pl.ds(0, 1)])
    for copy in top_copies:
        copy.wait()
    top = tops[0]
    for i in range(1, peaks):
        top = jnp.maximum(top, tops[i])
    envelope_out[...] = top
    dst_copy.wait()
    select = one_hot(iota((size.slots, size.convs), 0) == dst[...])
    received_copy.wait()
    parts = jnp.concatenate(split_3(received[...].T), axis=0)
    state = dot(parts, select)
    width = 2 * size.scen
    state = state[:width] + state[width : 2 * width] + state[2 * width :]
    state_out[0] = state[: size.scen]
    state_out[1] = state[size.scen :]
    newest_copy.wait()


def shape(dims, dtype=F32):
    return jax.ShapeDtypeStruct(dims, dtype)


def in_vmem(*values):
    return [pltpu.with_memory_space_constraint(v, pltpu.VMEM) for v in values]


def call(kernel, name, outs, out_specs, args, specs, scratch, limit, aliases=None):
    return pl.pallas_call(
        kernel,
        name=name,
        out_shape=outs,
        in_specs=specs,
        out_specs=out_specs,
        scratch_shapes=list(scratch),
        input_output_aliases=aliases or {},
        compiler_params=pltpu.CompilerParams(vmem_limit_bytes=limit << 20),
    )(*args)


def shards(
    inverse_blocks, block_cols, source_current, node_decay, node_gain, voltage_init, branch_init,
    wave_init, line_node, line_delay, line_admittance, conv_region, conv_node, conv_power,
    conv_gains, conv_init, fault_node, fault_kind,
):
    size = Sizes(inverse_blocks, voltage_init, wave_init, line_node, conv_node)
    regions, rows, scen = size.regions, size.rows, size.scen
    ring = [(i, (i + 1) % regions) for i in range(regions)]
    back_ring = [(j, i) for i, j in ring]
    dma = pltpu.SemaphoreType.DMA
    vmem = pltpu.VMEM

    def row(vector):
        return vector.reshape(1, -1)

    table = jnp.stack(
        [
            conv_region[:, 0].astype(F32),
            conv_power,
            conv_gains[0],
            conv_gains[1],
            conv_node.astype(F32),
        ]
    )
    table = jnp.concatenate([table, jnp.zeros((3, size.convs), F32)], axis=0)
    packed, dst = call(
        functools.partial(pack_kernel, size),
        "pack",
        [shape((regions, rows, 2 * scen)), shape((1, size.convs), I32)],
        [VMEM] * 2,
        [table, conv_init],
        [HBM] * 2,
        [vmem(table.shape, F32), vmem(conv_init.shape, F32), dma((2,))],
        16,
    )
    received = lax.all_to_all(packed, "region", split_axis=0, concat_axis=0, tiled=True)
    received = received.reshape(size.slots, 2 * scen)

    cols = block_cols.T
    cols_scratch = pltpu.SMEM(cols.shape, I32)
    x_scratch = vmem((size.blocks, 2 * scen, size.padded), BF)
    wide_scratch = vmem(size.wide, BF)
    kept = [
        (size.weights, BF),
        (size.site_rows, BF),
        (size.response, BF),
        (size.coupling, BF),
        (size.wide, BF),
        (size.state, F32),
        (size.state, F32),
        (size.node_rows, F32),
        (size.fault_cols, F32),
    ]
    vectors = (3, 1, size.nodes)
    args = [
        cols, inverse_blocks, row(source_current), row(node_decay), row(node_gain), voltage_init,
        branch_init, row(line_node), row(fault_node), row(fault_kind),
    ]
    wp_hbm, eg_hbm, mt_hbm, kk_hbm, vb_hbm, branch_hbm, rest_hbm, rows_hbm, fault_hbm = call(
        functools.partial(prep_kernel, size),
        "prep",
        [shape(*item) for item in kept],
        [HBM] * len(kept),
        args,
        [HBM] * len(args),
        [
            cols_scratch,
            vmem(inverse_blocks.shape, F32),
            vmem(vectors, F32),
            vmem(voltage_init.shape, F32),
            vmem(voltage_init.shape, F32),
            vmem((1, size.ends), I32),
            vmem((2, scen), I32),
            vmem(size.weights, BF),
            vmem(size.site_rows, BF),
            vmem((size.blocks, size.ends, size.padded), BF),
            vmem(size.response, BF),
            vmem((2 * size.ends, size.lanes), BF),
            vmem(size.coupling, BF),
            wide_scratch,
            vmem(size.state, F32),
            vmem(size.state, F32),
            vmem(size.state, F32),
            vmem(size.node_rows, F32),
            vmem(size.fault_cols, F32),
            dma((40,)),
        ],
        48,
    )

    slot_state = vmem((scen, size.slot_lanes), F32)
    outs = [
        vmem(size.weights, BF),
        vmem(size.site_rows, BF),
        vmem(size.response, BF),
        vmem(size.coupling, BF),
        vmem(wave_init.shape, F32),
        vmem((8, size.ends), F32),
        vmem(size.node_rows, F32),
        vmem(size.fault_cols, F32),
        vmem(size.state, F32),
        vmem((size.lanes, size.slot_lanes), BF),
        vmem((size.slot_lanes, size.lanes), BF),
        vmem((8, size.slot_lanes), F32),
        slot_state,
        slot_state,
        vmem(size.state, F32),
        vmem(size.node_rows, F32),
        vmem(size.drive, F32),
        shape(size.exchange),
        shape(size.exchange),
    ]
    args = [
        cols, received, wave_init, row(line_delay.astype(F32)), row(line_admittance), wp_hbm, eg_hbm,
        mt_hbm, kk_hbm, vb_hbm, branch_hbm, rest_hbm, rows_hbm, fault_hbm,
    ]
    (
        wp, eg, mt, kk, waves, ends, node_rows, fault_cols, branch, cg, cs, prm, filt, amps, volt,
        peak, drive, up, down,
    ) = call(
        functools.partial(start_kernel, size),
        "start",
        outs,
        [VMEM] * len(outs),
        args,
        [HBM] * len(args),
        [
            cols_scratch,
            vmem((size.slots, 2 * scen), F32),
            vmem((2, 1, size.ends), F32),
            vmem(size.state, F32),
            x_scratch,
            wide_scratch,
            dma((16,)),
        ],
        10,
    )

    arrivals = []
    for step in range(1, STEPS):
        last = step == STEPS - 1
        from_ahead = lax.ppermute(up, "region", ring)
        from_after = lax.ppermute(down, "region", back_ring)
        outs = [
            vmem(size.state, F32),
            slot_state,
            slot_state,
            vmem(size.state, F32),
            vmem(size.node_rows, F32),
            vmem(size.drive, F32),
        ]
        if last:
            outs += [vmem((size.slots, 2 * scen), F32), shape((scen, size.nodes))]
        result = call(
            functools.partial(middle_kernel, size, last),
            "middle",
            outs,
            [VMEM] * len(outs),
            [cols]
            + in_vmem(
                drive, wp, eg, mt, node_rows, fault_cols, cg, cs, prm, branch, filt, amps, volt, peak
            ),
            [HBM] + [VMEM] * 14,
            [cols_scratch, x_scratch, wide_scratch, dma],
            8,
            {10: 0, 11: 1, 12: 2, 13: 3, 14: 4},
        )
        branch, filt, amps, volt, peak, at_ends = result[:6]
        arrivals = [from_ahead, from_after] + arrivals
        args = in_vmem(at_ends, kk, ends, waves) + arrivals
        outs = [vmem(size.drive, F32), shape(size.exchange), shape(size.exchange)]
        specs, scratch = [VMEM] * 3, []
        if last:
            back, branch_out = result[6:]
            args += in_vmem(back)
            outs[0] = shape(size.drive)
            outs += [shape((size.slots, 2 * scen)), shape(wave_init.shape)]
            specs += [HBM, HBM]
            scratch = [vmem((step, *size.drive), F32), dma((3,))]
        drive, up, down, *rest = call(
            functools.partial(launch_kernel, size, step, last),
            "launch",
            outs,
            specs,
            args,
            [VMEM] * len(args),
            scratch,
            4,
        )
    chunks, waves_out = rest
    from_ahead = lax.ppermute(up, "region", ring)
    from_after = lax.ppermute(down, "region", back_ring)
    chunks = chunks.reshape(regions, rows, 2 * scen)
    returned = lax.all_to_all(chunks, "region", split_axis=0, concat_axis=0, tiled=True)
    voltage_out, peak_out = call(
        functools.partial(final_kernel, size),
        "final",
        [shape((scen, size.nodes)), shape((1, size.nodes))],
        [VMEM] * 2,
        [drive, volt, mt_hbm, peak],
        [VMEM, HBM, HBM, HBM],
        [
            vmem(size.state, F32),
            vmem(size.response, BF),
            vmem(size.node_rows, F32),
            dma((5,)),
        ],
        12,
    )
    others = lax.axis_size("scen")
    peaks = [peak_out] + [
        lax.ppermute(peak_out, "scen", [(i, (i + d) % others) for i in range(others)])
        for d in range(1, others)
    ]
    returned = returned.reshape(size.slots, 2 * scen)
    args = [dst, returned, from_ahead, from_after, waves_out] + peaks
    conv_state, wave_history, envelope = call(
        functools.partial(end_kernel, size, len(peaks)),
        "end",
        [shape(conv_init.shape), shape(wave_init.shape), shape((1, size.nodes))],
        [VMEM, HBM, VMEM],
        args,
        [HBM, HBM, VMEM, VMEM] + [HBM] * (len(args) - 4),
        [
            vmem(dst.shape, I32),
            vmem(returned.shape, F32),
            vmem((1, *size.drive), F32),
            vmem((others, 1, size.nodes), F32),
            dma((3 + others,)),
        ],
        16,
        {4: 1},
    )
    return voltage_out, branch_out, wave_history, conv_state, envelope.reshape(-1)


def solution(mesh):
    placed = (
        P("region", None, None, None),
        P("region", None),
        P("region"),
        P("region"),
        P("region"),
        P("scen", "region"),
        P("scen", "region"),
        P(None, "scen", "region"),
        P("region"),
        P("region"),
        P("region"),
        P("region", None),
        P("region"),
        P("region"),
        P(None, "region"),
        P(None, "scen", "region"),
        P("scen"),
        P("scen"),
    )
    return jax.shard_map(
        shards,
        mesh=mesh,
        in_specs=placed,
        out_specs=(
            P("scen", "region"),
            P("scen", "region"),
            P(None, "scen", "region"),
            P(None, "scen", "region"),
            P("region"),
        ),
        check_vma=False,
    )
```

time: 133 us -> 130 us (0.977)
  blocking collectives: 20.9 us -> 0 us
  waiting for transfers between devices: 15.1 us -> 2.98 us
  starting transfers between devices: 19.6 us -> 31.6 us
  Pallas kernels: 51.5 us -> 60.7 us
  local copies, waits for them, and re-layouts: 23.4 us -> 30.6 us
  other arithmetic: 0 us -> 2.1 us
    all_to_all x1 -> x0, blocking collectives: 20.9 us -> none  [shards(): lax.all_to_all(packed, 'region', split_axis=0, concat_axis=0, tiled=True)]
    all_to_all x1, waiting for transfers between devices: 12.2 us -> 0.01 us  [shards(): lax.all_to_all(chunks, 'region', split_axis=0, concat_axis=0, tiled=True)]
    pallas_call x9 -> x11, Pallas kernels: 51.5 us -> 60.7 us  [call(): pl.pallas_call(kernel, name=name, out_shape=outs, in_specs=specs, out_spe...]
    all_to_all x0 -> x1, starting transfers between devices: none -> 7.29 us  [shards(): lax.all_to_all(packed, 'region', split_axis=0, concat_axis=0, tiled=True)]
    unnamed x72 -> x52, local copies, waits for them, and re-layouts: 22 us -> 29.2 us
    ppermute x3 -> x4, starting transfers between devices: 1.62 us -> 4.04 us  [shards(): from_ahead = lax.ppermute(up, 'region', ring)]
    ppermute x3 -> x4, starting transfers between devices: 12.7 us -> 15 us  [shards(): from_after = lax.ppermute(down, 'region', back_ring)]
    convert_element_type x0 -> x3, other arithmetic: none -> 2.1 us  [the longest x1 0.74 us: shards(): conv_region[:, 0].astype(F32)]
  transfers between devices with their start and end apart: 10 -> 13, of which waited for: 3 -> 2; matrix products, arithmetic and copies ran while one was open for 0% -> 1% of each run, Pallas kernels for 11% -> 32%
where the time goes in v1:
time: 130 us; the launch traced here: 129 us
  Pallas kernels  60.7 us (47%)
  starting transfers between devices  31.6 us (24%)
  local copies, waits for them, and re-layouts  30.6 us (24%)
  waiting for transfers between devices  2.98 us (2%)
  other arithmetic  2.1 us (2%)
    pallas_call x11, Pallas kernels, call(): pl.pallas_call(kernel, name=name, out_shape=outs, in_specs=specs, out_spe...  60.7 us
    unnamed x52, local copies, waits for them, and re-layouts  29.2 us
    ppermute x4, starting transfers between devices, shards(): from_after = lax.ppermute(down, 'region', back_ring)  15 us
    all_to_all x1, starting transfers between devices, shards(): lax.all_to_all(packed, 'region', split_axis=0, concat_axis=0, tiled=True)  7.29 us
    ppermute x4, starting transfers between devices, shards(): from_ahead = lax.ppermute(up, 'region', ring)  4.04 us
    all_to_all x1, starting transfers between devices, shards(): lax.all_to_all(chunks, 'region', split_axis=0, concat_axis=0, tiled=True)  3.49 us
    ppermute x3, waiting for transfers between devices, shards(): lax.ppermute(peak_out, 'scen', [(i, (i + d) % others) for i in range(othe...  2.95 us
  transfers between devices with their start and end apart: 13, of which 2 were waited for; matrix products, arithmetic and copies ran while one was open for 1% of the time, Pallas kernels for 32%

profile of v1, /device:TPU:0, one launch (start us, length us, event | category | flops | bytes accessed | tf_op | source)
XLA Modules:
  0.0 129.0 jit_solution(2493347557521752452)
XLA Ops:
  4.4 2.5 %pack.1 = (f32[8,120,128]{2,1,0:T(8,128)}, s32[1,384]{1,0:T(1,128)S(1)}) custom-call(f32[8,384]{1,0:T(8,128)S(1)} %concatenate.3.table_hbm, f32[2,64,384]{2,1,0:T(8,128)S(1)} %copy-done.16), custom_call_target="tpu_custom_call" | custom-call | tf_op jit(solution)/shard_map/pack/pallas_call | solution.py:530
  6.9 7.3 %all-to-all-start = ((f32[8,120,128]{2,1,0:T(8,128)}), f32[8,120,128]{2,1,0:T(8,128)S(1)}, u32[]{:S(2)}, u32[]{:S(2)}) async-start(f32[8,120,128]{2,1,0:T(8,128)} %get-tuple-element.68), calls=%async_computation | async-start | bytes 983040 | tf_op jit(solution)/shard_map/all_to_all | solution.py:577
  14.9 1.1 copy-done.11
  16.0 1.1 copy-done.12
  21.9 13.2 %prep.1 = (bf16[32,480,256]{2,1,0:T(8,128)(2,1)}, bf16[4096,256]{1,0:T(8,128)(2,1)}, bf16[32,256,256]{2,1,0:T(8,128)(2,1)}, bf16[256,512]{1,0:T(8,128)(2,1)S(1)}...) custom-call(s32[5,32]{1,0:T(8,128)S(1)} %bitcast.17, ...), custom_call_target="tpu_custom_call" | custom-call | tf_op jit(solution)/shard_map/prep/pallas_call | solution.py:530
  35.1 1.0 copy-done.5
  36.1 1.0 copy-done.7
  37.1 1.0 copy-done.9
  38.8 2.2 %copy-done.2 = bf16[32,256,256]{2,1,0:T(8,128)(2,1)S(1)} copy-done((bf16[32,256,256]{2,1,0:T(8,128)(2,1)S(1)}, bf16[32,256,256]{2,1,0:T(8,128)(2,1)}, u32[]{:S(2)}) %copy-start.2) | copy-done | bytes 4194328
  41.0 1.6 %copy-done.4 = bf16[4096,256]{1,0:T(8,128)(2,1)S(1)} copy-done((bf16[4096,256]{1,0:T(8,128)(2,1)S(1)}, bf16[4096,256]{1,0:T(8,128)(2,1)}, u32[]{:S(2)}) %copy-start.4) | copy-done | bytes 2097176
  42.5 1.2 copy-done.6
  43.8 1.2 copy-done.8
  45.0 1.2 copy-done.10
  47.8 14.2 %start.1 = (bf16[32,480,256]{2,1,0:T(8,128)(2,1)S(1)}, bf16[4096,256]{1,0:T(8,128)(2,1)S(1)}, bf16[32,256,256]{2,1,0:T(8,128)(2,1)S(1)}, bf16[256,512]{1,0:T(8,1...) custom-call(s32[5,32]{1,0:T(8,128)S(1)} %bitcast.18, ...), custom_call_target="tpu_custom_call" | custom-call | tf_op jit(solution)/shard_map/start/pallas_call | solution.py:530
  62.1 3.1 %copy-done = bf16[32,480,256]{2,1,0:T(8,128)(2,1)} copy-done((bf16[32,480,256]{2,1,0:T(8,128)(2,1)}, bf16[32,480,256]{2,1,0:T(8,128)(2,1)S(1)}, u32[]{:S(2)}) %copy-start) | copy-done | bytes 7864344
  65.2 2.0 %collective-permute-start = (f32[64,128]{1,0:T(8,128)S(1)}, f32[64,128]{1,0:T(8,128)S(1)}, u32[]{:S(2)}, u32[]{:S(2)}) collective-permute-start(f32[64,128]{1,0:T(8,128)S(1)} %get-tuple-element.96), channel_id=1, source_target_pairs={{0,4},{4,8},{8,12},{12,16},{16,20},{20,24},{24,28},{28,0},{1,5},{5... | collective-permute-start | bytes 98312 | tf_op jit(solution)/shard_map/ppermute | solution.py:683
  67.2 2.7 %collective-permute-start.1 = (f32[64,128]{1,0:T(8,128)S(1)}, f32[64,128]{1,0:T(8,128)S(1)}, u32[]{:S(2)}, u32[]{:S(2)}) collective-permute-start(f32[64,128]{1,0:T(8,128)S(1)} %get-tuple-element.97), channel_id=1, source_target_pairs={{4,0},{8,4},{12,8},{16,12},{20,16},{24,20},{28,24},{0,28},{5,1},{9... | collective-permute-start | bytes 98312 | tf_op jit(solution)/shard_map/ppermute | solution.py:684
  69.9 3.2 %copy-done.1 = bf16[32,480,256]{2,1,0:T(8,128)(2,1)S(1)} copy-done((bf16[32,480,256]{2,1,0:T(8,128)(2,1)S(1)}, bf16[32,480,256]{2,1,0:T(8,128)(2,1)}, u32[]{:S(2)}) %copy-start.1) | copy-done | bytes 7864344
  73.1 8.1 %middle.3 = (f32[32,64,128]{2,1,0:T(8,128)S(1)}, f32[64,1024]{1,0:T(8,128)S(1)}, f32[64,1024]{1,0:T(8,128)S(1)}, f32[32,64,128]{2,1,0:T(8,128)S(1)}, f32[32,8,128]{2,1,0:T(8,128)S(1)}, /*index=5*/f32[64,256]{1,0:T(8,128)S(1)}) custom-call(s32[5,32]{1,0:T(8,128)S(1)} %bitcast.19, ...), custom_call_target="tpu_custom_call", output_to_operand_aliasing={{0}: (10, {}), {1}: (11, {}), {2}: (12, {}), {3}: (13, {}),... | custom-call | tf_op jit(solution)/shard_map/middle/pallas_call | solution.py:530
  81.5 4.7 %collective-permute-start.3 = (f32[64,128]{1,0:T(8,128)S(1)}, f32[64,128]{1,0:T(8,128)S(1)}, u32[]{:S(2)}, u32[]{:S(2)}) collective-permute-start(f32[64,128]{1,0:T(8,128)S(1)} %get-tuple-element.106), channel_id=1, source_target_pairs={{4,0},{8,4},{12,8},{16,12},{20,16},{24,20},{28,24},{0,28},{5,1},{9... | collective-permute-start | bytes 98312 | tf_op jit(solution)/shard_map/ppermute | solution.py:684
  86.2 8.1 %middle.4 = (f32[32,64,128]{2,1,0:T(8,128)S(1)}, f32[64,1024]{1,0:T(8,128)S(1)}, f32[64,1024]{1,0:T(8,128)S(1)}, f32[32,64,128]{2,1,0:T(8,128)S(1)}, f32[32,8,128]{2,1,0:T(8,128)S(1)}, /*index=5*/f32[64,256]{1,0:T(8,128)S(1)}) custom-call(s32[5,32]{1,0:T(8,128)S(1)} %bitcast.20, ...), custom_call_target="tpu_custom_call", output_to_operand_aliasing={{0}: (10, {}), {1}: (11, {}), {2}: (12, {}), {3}: (13, {}),... | custom-call | tf_op jit(solution)/shard_map/middle/pallas_call | solution.py:530
  94.5 4.7 %collective-permute-start.5 = (f32[64,128]{1,0:T(8,128)S(1)}, f32[64,128]{1,0:T(8,128)S(1)}, u32[]{:S(2)}, u32[]{:S(2)}) collective-permute-start(f32[64,128]{1,0:T(8,128)S(1)} %get-tuple-element.115), channel_id=1, source_target_pairs={{4,0},{8,4},{12,8},{16,12},{20,16},{24,20},{28,24},{0,28},{5,1},{9... | collective-permute-start | bytes 98312 | tf_op jit(solution)/shard_map/ppermute | solution.py:684
  99.3 9.0 %middle.5 = (f32[32,64,128]{2,1,0:T(8,128)S(1)}, f32[64,1024]{1,0:T(8,128)S(1)}, f32[64,1024]{1,0:T(8,128)S(1)}, f32[32,64,128]{2,1,0:T(8,128)S(1)}, f32[32,8,12...) custom-call(s32[5,32]{1,0:T(8,128)S(1)} %bitcast.21, ...), custom_call_target="tpu_custom_call", output_to_operand_aliasing={{0}: (10, {}), {1}: (11, {}), {2}: (12, {}), {3}: (13, {}),... | custom-call | tf_op jit(solution)/shard_map/middle/pallas_call | solution.py:530
  108.3 1.0 launch.5
  109.3 3.5 %all-to-all-start.1 = ((f32[8,120,128]{2,1,0:T(8,128)}), f32[8,120,128]{2,1,0:T(8,128)S(1)}, u32[]{:S(2)}, u32[]{:S(2)}) async-start(f32[8,120,128]{2,1,0:T(8,128)} %bitcast.11), calls=%async_computation.1 | async-start | bytes 983040 | tf_op jit(solution)/shard_map/all_to_all | solution.py:735
  112.8 1.9 %collective-permute-start.6 = (f32[64,128]{1,0:T(8,128)S(1)}, f32[64,128]{1,0:T(8,128)S(1)}, u32[]{:S(2)}, u32[]{:S(2)}) collective-permute-start(f32[64,128]{1,0:T(8,128)S(1)} %get-tuple-element.124), channel_id=1, source_target_pairs={{0,4},{4,8},{8,12},{12,16},{16,20},{20,24},{24,28},{28,0},{1,5},{5... | collective-permute-start | bytes 98312 | tf_op jit(solution)/shard_map/ppermute | solution.py:732
  114.7 2.9 %collective-permute-start.7 = (f32[64,128]{1,0:T(8,128)S(1)}, f32[64,128]{1,0:T(8,128)S(1)}, u32[]{:S(2)}, u32[]{:S(2)}) collective-permute-start(f32[64,128]{1,0:T(8,128)S(1)} %get-tuple-element.125), channel_id=1, source_target_pairs={{4,0},{8,4},{12,8},{16,12},{20,16},{24,20},{28,24},{0,28},{5,1},{9... | collective-permute-start | bytes 98312 | tf_op jit(solution)/shard_map/ppermute | solution.py:733
  117.5 2.2 %copy-done.3 = bf16[32,256,256]{2,1,0:T(8,128)(2,1)S(1)} copy-done((bf16[32,256,256]{2,1,0:T(8,128)(2,1)S(1)}, bf16[32,256,256]{2,1,0:T(8,128)(2,1)}, u32[]{:S(2)}) %copy-start.3) | copy-done | bytes 4194328
  119.7 2.4 %final.1 = (f32[64,3072]{1,0:T(8,128)}, f32[1,3072]{1,0:T(1,128)S(1)}) custom-call(f32[64,256]{1,0:T(8,128)S(1)} %get-tuple-element.117.drive, f32[32,64,128]{2,1,0:T(8,128)S(1)} %get-tuple-element.118.volt_hbm, bf16[32,256,256]{2,1,0:T(8,128)(2,1)S(1)} %copy-done.3, f32[32,8,128]{2,1,0:T(8,128)S(1)} %get-tuple-element.119.peak_hbm), custom_call_target="tpu_custom_call" | custom-call | tf_op jit(solution)/shard_map/final/pallas_call | solution.py:530
  122.2 1.6 %collective-permute-start.9 = (f32[1,3072]{1,0:T(1,128)S(1)}, f32[1,3072]{1,0:T(1,128)S(1)}, u32[]{:S(2)}, u32[]{:S(2)}) collective-permute-start(f32[1,3072]{1,0:T(1,128)S(1)} %get-tuple-element.127.refs_0_), channel_id=1, source_target_pairs={{0,2},{1,3},{2,0},{3,1},{4,6},{5,7},{6,4},{7,5},{8,10},{9,11},{10,... | collective-permute-start | bytes 36872 | tf_op jit(solution)/shard_map/ppermute | solution.py:753
  123.9 2.0 %collective-permute-done.9.refs_2_ = f32[1,3072]{1,0:T(1,128)S(1)} collective-permute-done((f32[1,3072]{1,0:T(1,128)S(1)}, f32[1,3072]{1,0:T(1,128)S(1)}, u32[]{:S(2)}, u32[]{:S(2)}) %collective-permute-start.9) | collective-permute-done | bytes 12320 | tf_op jit(solution)/shard_map/ppermute | solution.py:753
  126.9 1.9 %end.1 = (f32[2,64,384]{2,1,0:T(8,128)}, f32[8,64,256]{2,1,0:T(8,128)}, f32[1,3072]{1,0:T(1,128)}) custom-call(s32[1,384]{1,0:T(1,128)S(1)} %get-tuple-element.122.dst_hbm, f32[960,128]{1,0:T(8,128)S(1)} %bitcast.15, f32[64,128]{1,0:T(8,128)S(1)} %collective-permute-done.6.ahead, ...), custom_call_target="tpu_custom_call", output_to_operand_aliasing={{1}: (4, {})} | custom-call | tf_op jit(solution)/shard_map/end/pallas_call | solution.py:530
  (64 shorter events, 13.3 us)
Async XLA Ops:
  0.6 38.1 %copy-start.13 = (f32[8,64,256]{2,1,0:T(8,128)S(1)}, f32[8,64,256]{2,1,0:T(8,128)}, u32[]{:S(2)}) copy-start(f32[8,64,256]{2,1,0:T(8,128)} %waves_hbm.1) | copy-start | bytes 1572868
  3.5 0.9 copy-start.16
  4.4 34.4 %copy-start.18 = (s32[32,5]{0,1:T(8,128)S(1)}, s32[32,5]{0,1:T(8,128)}, u32[]{:S(2)}) copy-start(s32[32,5]{0,1:T(8,128)} %param.19) | copy-start | bytes 1924
  6.9 31.9 %all-to-all-start = ((f32[8,120,128]{2,1,0:T(8,128)}), f32[8,120,128]{2,1,0:T(8,128)S(1)}, u32[]{:S(2)}, u32[]{:S(2)}) async-start(f32[8,120,128]{2,1,0:T(8,128)} %get-tuple-element.68), calls=%async_computation | async-start | bytes 983040 | tf_op jit(solution)/shard_map/all_to_all | solution.py:577
  14.9 1.1 copy-start.11
  16.0 1.1 copy-start.12
  17.8 0.7 copy-start.19
  18.5 0.7 copy-start.20
  35.1 1.0 copy-start.5
  36.1 1.0 copy-start.7
  37.1 1.0 copy-start.9
  38.8 2.2 %copy-start.2 = (bf16[32,256,256]{2,1,0:T(8,128)(2,1)S(1)}, bf16[32,256,256]{2,1,0:T(8,128)(2,1)}, u32[]{:S(2)}) copy-start(bf16[32,256,256]{2,1,0:T(8,128)(2,1)} %get-tuple-element.71.mt_hbm) | copy-start | bytes 12582916
  41.0 1.6 %copy-start.4 = (bf16[4096,256]{1,0:T(8,128)(2,1)S(1)}, bf16[4096,256]{1,0:T(8,128)(2,1)}, u32[]{:S(2)}) copy-start(bf16[4096,256]{1,0:T(8,128)(2,1)} %get-tuple-element.70.eg_hbm) | copy-start | bytes 6291460
  42.5 1.2 copy-start.6
  43.8 1.2 copy-start.8
  45.0 1.2 copy-start.10
  46.2 0.9 copy-start.15
  62.1 3.1 %copy-start = (bf16[32,480,256]{2,1,0:T(8,128)(2,1)}, bf16[32,480,256]{2,1,0:T(8,128)(2,1)S(1)}, u32[]{:S(2)}) copy-start(bf16[32,480,256]{2,1,0:T(8,128)(2,1)S(1)} %get-tuple-element.79.wp) | copy-start | bytes 23592964
  65.2 16.0 %collective-permute-start = (f32[64,128]{1,0:T(8,128)S(1)}, f32[64,128]{1,0:T(8,128)S(1)}, u32[]{:S(2)}, u32[]{:S(2)}) collective-permute-start(f32[64,128]{1,0:T(8,128)S(1)} %get-tuple-element.96), channel_id=1, source_target_pairs={{0,4},{4,8},{8,12},{12,16},{16,20},{20,24},{24,28},{28,0},{1,5},{5... | collective-permute-start | bytes 98312 | tf_op jit(solution)/shard_map/ppermute | solution.py:683
  67.2 14.0 %collective-permute-start.1 = (f32[64,128]{1,0:T(8,128)S(1)}, f32[64,128]{1,0:T(8,128)S(1)}, u32[]{:S(2)}, u32[]{:S(2)}) collective-permute-start(f32[64,128]{1,0:T(8,128)S(1)} %get-tuple-element.97), channel_id=1, source_target_pairs={{4,0},{8,4},{12,8},{16,12},{20,16},{24,20},{28,24},{0,28},{5,1},{9... | collective-permute-start | bytes 98312 | tf_op jit(solution)/shard_map/ppermute | solution.py:684
  69.9 3.2 %copy-start.1 = (bf16[32,480,256]{2,1,0:T(8,128)(2,1)S(1)}, bf16[32,480,256]{2,1,0:T(8,128)(2,1)}, u32[]{:S(2)}) copy-start(bf16[32,480,256]{2,1,0:T(8,128)(2,1)} %copy-done) | copy-start | bytes 23592964
  81.4 12.8 %collective-permute-start.2 = (f32[64,128]{1,0:T(8,128)S(1)}, f32[64,128]{1,0:T(8,128)S(1)}, u32[]{:S(2)}, u32[]{:S(2)}) collective-permute-start(f32[64,128]{1,0:T(8,128)S(1)} %get-tuple-element.105), channel_id=1, source_target_pairs={{0,4},{4,8},{8,12},{12,16},{16,20},{20,24},{24,28},{28,0},{1,5},{5... | collective-permute-start | bytes 98312 | tf_op jit(solution)/shard_map/ppermute | solution.py:683
  81.5 12.8 %collective-permute-start.3 = (f32[64,128]{1,0:T(8,128)S(1)}, f32[64,128]{1,0:T(8,128)S(1)}, u32[]{:S(2)}, u32[]{:S(2)}) collective-permute-start(f32[64,128]{1,0:T(8,128)S(1)} %get-tuple-element.106), channel_id=1, source_target_pairs={{4,0},{8,4},{12,8},{16,12},{20,16},{24,20},{28,24},{0,28},{5,1},{9... | collective-permute-start | bytes 98312 | tf_op jit(solution)/shard_map/ppermute | solution.py:684
  94.5 13.8 %collective-permute-start.4 = (f32[64,128]{1,0:T(8,128)S(1)}, f32[64,128]{1,0:T(8,128)S(1)}, u32[]{:S(2)}, u32[]{:S(2)}) collective-permute-start(f32[64,128]{1,0:T(8,128)S(1)} %get-tuple-element.114), channel_id=1, source_target_pairs={{0,4},{4,8},{8,12},{12,16},{16,20},{20,24},{24,28},{28,0},{1,5},{5... | collective-permute-start | bytes 98312 | tf_op jit(solution)/shard_map/ppermute | solution.py:683
  94.5 13.7 %collective-permute-start.5 = (f32[64,128]{1,0:T(8,128)S(1)}, f32[64,128]{1,0:T(8,128)S(1)}, u32[]{:S(2)}, u32[]{:S(2)}) collective-permute-start(f32[64,128]{1,0:T(8,128)S(1)} %get-tuple-element.115), channel_id=1, source_target_pairs={{4,0},{8,4},{12,8},{16,12},{20,16},{24,20},{28,24},{0,28},{5,1},{9... | collective-permute-start | bytes 98312 | tf_op jit(solution)/shard_map/ppermute | solution.py:684
  109.3 17.6 %all-to-all-start.1 = ((f32[8,120,128]{2,1,0:T(8,128)}), f32[8,120,128]{2,1,0:T(8,128)S(1)}, u32[]{:S(2)}, u32[]{:S(2)}) async-start(f32[8,120,128]{2,1,0:T(8,128)} %bitcast.11), calls=%async_computation.1 | async-start | bytes 983040 | tf_op jit(solution)/shard_map/all_to_all | solution.py:735
  112.8 14.1 %collective-permute-start.6 = (f32[64,128]{1,0:T(8,128)S(1)}, f32[64,128]{1,0:T(8,128)S(1)}, u32[]{:S(2)}, u32[]{:S(2)}) collective-permute-start(f32[64,128]{1,0:T(8,128)S(1)} %get-tuple-element.124), channel_id=1, source_target_pairs={{0,4},{4,8},{8,12},{12,16},{16,20},{20,24},{24,28},{28,0},{1,5},{5... | collective-permute-start | bytes 98312 | tf_op jit(solution)/shard_map/ppermute | solution.py:732
  114.7 12.2 %collective-permute-start.7 = (f32[64,128]{1,0:T(8,128)S(1)}, f32[64,128]{1,0:T(8,128)S(1)}, u32[]{:S(2)}, u32[]{:S(2)}) collective-permute-start(f32[64,128]{1,0:T(8,128)S(1)} %get-tuple-element.125), channel_id=1, source_target_pairs={{4,0},{8,4},{12,8},{16,12},{20,16},{24,20},{28,24},{0,28},{5,1},{9... | collective-permute-start | bytes 98312 | tf_op jit(solution)/shard_map/ppermute | solution.py:733
  117.5 2.2 %copy-start.3 = (bf16[32,256,256]{2,1,0:T(8,128)(2,1)S(1)}, bf16[32,256,256]{2,1,0:T(8,128)(2,1)}, u32[]{:S(2)}) copy-start(bf16[32,256,256]{2,1,0:T(8,128)(2,1)} %get-tuple-element.71.mt_hbm) | copy-start | bytes 12582916
  122.1 1.8 %collective-permute-start.10 = (f32[1,3072]{1,0:T(1,128)S(1)}, f32[1,3072]{1,0:T(1,128)S(1)}, u32[]{:S(2)}, u32[]{:S(2)}) collective-permute-start(f32[1,3072]{1,0:T(1,128)S(1)} %get-tuple-element.127.refs_0_), channel_id=1, source_target_pairs={{0,3},{1,0},{2,1},{3,2},{4,7},{5,4},{6,5},{7,6},{8,11},{9,8},{10,9... | collective-permute-start | bytes 36872 | tf_op jit(solution)/shard_map/ppermute | solution.py:753
  122.2 3.8 %collective-permute-start.9 = (f32[1,3072]{1,0:T(1,128)S(1)}, f32[1,3072]{1,0:T(1,128)S(1)}, u32[]{:S(2)}, u32[]{:S(2)}) collective-permute-start(f32[1,3072]{1,0:T(1,128)S(1)} %get-tuple-element.127.refs_0_), channel_id=1, source_target_pairs={{0,2},{1,3},{2,0},{3,1},{4,6},{5,7},{6,4},{7,5},{8,10},{9,11},{10,... | collective-permute-start | bytes 36872 | tf_op jit(solution)/shard_map/ppermute | solution.py:753
  123.8 3.1 %collective-permute-start.8 = (f32[1,3072]{1,0:T(1,128)S(1)}, f32[1,3072]{1,0:T(1,128)S(1)}, u32[]{:S(2)}, u32[]{:S(2)}) collective-permute-start(f32[1,3072]{1,0:T(1,128)S(1)} %get-tuple-element.127.refs_0_), channel_id=1, source_target_pairs={{0,1},{1,2},{2,3},{3,0},{4,5},{5,6},{6,7},{7,4},{8,9},{9,10},{10,1... | collective-permute-start | bytes 36872 | tf_op jit(solution)/shard_map/ppermute | solution.py:753
  (7 other events, 4.8 us)

commit v2 on v1

--- a/solution.py
+++ b/solution.py
@@ -125,13 +125,17 @@
     return slice(b * size.padded, (b + 1) * size.padded)
 
 
-def pack_kernel(size, table_hbm, init_hbm, out, dst_out, table, init, sems):
+def pack_kernel(
+    size, region_hbm, table_hbm, gains_hbm, init_hbm, out_hbm, dst_hbm,
+    region, table, gains, init, out, dst_out, sems,
+):
     convs, slots = size.convs, size.slots
     copies = Copies(sems)
-    first = copies.start(table_hbm, table)
+    first = copies.start(region_hbm, region)
     second = copies.start(init_hbm, init)
+    others = [copies.start(table_hbm, table), copies.start(gains_hbm, gains)]
     first.wait()
-    target = table[0:1, :].astype(I32)
+    target = region[...]
     member = iota((round_up(size.regions, 16), convs), 0) == target
     before = one_hot(iota((convs, convs), 0) < iota((convs, convs), 1))
     earlier = dot(one_hot(member), before)
@@ -139,7 +143,12 @@
     dst = target * size.rows + rank.astype(I32)
     dst_out[...] = dst
     select = one_hot(iota((slots, convs), 0) == dst)
-    settings = jnp.concatenate([table[1:5, :], jnp.zeros((LANES - 4, convs), F32)], axis=0)
+    sent = [copies.start(dst_out, dst_hbm)]
+    for copy in others:
+        copy.wait()
+    settings = jnp.concatenate(
+        [table[0:1, :], gains[...], table[1:2, :], jnp.zeros((LANES - 4, convs), F32)], axis=0
+    )
     second.wait()
     state = jnp.concatenate([init[0], init[1]], axis=0)
     payload = jnp.concatenate([state.T, settings.T], axis=1)
@@ -151,6 +160,9 @@
         filler = jnp.zeros((LANES - size.rows, LANES), F32)
         turned = jnp.concatenate([chunk[:, width:], filler], axis=0).T
         out[r, size.capacity : size.capacity + 4, :] = turned[:4]
+    sent.append(copies.start(out, out_hbm))
+    for copy in sent:
+        copy.wait()
 
 
 def fault_terms(size, node, kind):
@@ -167,6 +179,22 @@
         return jnp.broadcast_to(jnp.sum(spread, axis=1, keepdims=True), (size.scen, size.padded))
 
     return column(site), column(level)
+
+
+def site_products(size, row, chunk, gather, scatter):
+    part = row[:, chunk : chunk + LANES]
+    block = jnp.floor((part + 0.5) * (1.0 / LANES))
+    lane = part - block * LANES
+    square = (LANES, LANES)
+    down_block = jnp.broadcast_to(block, square).astype(BF)
+    across_block = turned_row(block).astype(BF)
+    down_lane = one_hot(lane == iota(square, 0).astype(F32))
+    across_lane = one_hot(turned_row(lane) == iota(square, 1).astype(F32))
+    zeros = jnp.zeros(square, BF)
+    for n in range(size.lanes // LANES):
+        here = jnp.asarray(n, BF)
+        gather(n, jnp.where(down_block == here, down_lane, zeros))
+        scatter(n, jnp.where(across_block == here, across_lane, zeros))
 
 
 def turned_row(row):
@@ -226,13 +254,14 @@
 
     row = padded_index(nodes[...].astype(F32), size.width, size.padded)
     for c in range(0, size.ends, LANES):
-        part = row[:, c : c + LANES]
-        down_delta = part - iota((LANES, LANES), 0).astype(F32)
-        across_delta = turned_row(part) - iota((LANES, LANES), 1).astype(F32)
-        for n in range(0, size.lanes, LANES):
-            eg[n : n + LANES, c : c + LANES] = one_hot(down_delta == float(n))
-            b, lane = n // size.padded, n % size.padded
-            es[b, c : c + LANES, lane : lane + LANES] = one_hot(across_delta == float(n))
+        def put_gather(n, value, c=c):
+            eg[n * LANES : (n + 1) * LANES, c : c + LANES] = value
+
+        def put_scatter(n, value, c=c):
+            b, lane = n * LANES // size.padded, n * LANES % size.padded
+            es[b, c : c + LANES, lane : lane + LANES] = value
+
+        site_products(size, row, c, put_gather, put_scatter)
     sent.append(copies.start(eg, eg_out))
 
     for i in range(3):
@@ -333,7 +362,7 @@
     wp_hbm, eg_hbm, mt_hbm, kk_hbm, vb_hbm, branch_hbm, rest_hbm, rows_hbm, fault_hbm,
     wp, eg, mt, kk, waves, ends, node_rows, fault_cols, branch, cg, cs, prm, filt, amps, volt,
     peak, drive, up, down,
-    cols, received, line_rows, rest, x, vb, sems,
+    cols, received, delays, admittances, rest, x, vb, sems,
 ):
     copies = Copies(sems)
     received_copy = copies.start(received_hbm, received)
@@ -343,8 +372,8 @@
     wp_copy = copies.start(wp_hbm, wp)
     later = [
         copies.start(eg_hbm, eg),
-        copies.start(delay_hbm, line_rows.at[0]),
-        copies.start(admittance_hbm, line_rows.at[1]),
+        copies.start(delay_hbm, delays),
+        copies.start(admittance_hbm, admittances),
         copies.start(waves_hbm, waves),
         copies.start(kk_hbm, kk),
         copies.start(mt_hbm, mt),
@@ -372,12 +401,13 @@
         amps[:, c : c + LANES] = turned[size.scen :]
     row = padded_index(prm[3:4, :], size.width, size.padded)
     for c in range(0, size.slot_lanes, LANES):
-        part = row[:, c : c + LANES]
-        down_delta = part - iota((LANES, LANES), 0).astype(F32)
-        across_delta = turned_row(part) - iota((LANES, LANES), 1).astype(F32)
-        for n in range(0, size.lanes, LANES):
-            cg[n : n + LANES, c : c + LANES] = one_hot(down_delta == float(n))
-            cs[c : c + LANES, n : n + LANES] = one_hot(across_delta == float(n))
+        def put_gather(n, value, c=c):
+            cg[n * LANES : (n + 1) * LANES, c : c + LANES] = value
+
+        def put_scatter(n, value, c=c):
+            cs[c : c + LANES, n * LANES : (n + 1) * LANES] = value
+
+        site_products(size, row, c, put_gather, put_scatter)
     peak[...] = jnp.zeros(peak.shape, F32)
 
     vb_copy.wait()
@@ -391,8 +421,8 @@
     apply_inverse(size, cols, x, wp, volt, vb)
     for copy in later:
         copy.wait()
-    ends[0:1, :] = line_rows[0].astype(F32)
-    ends[1:2, :] = line_rows[1]
+    ends[0:1, :] = delays[...].astype(F32)
+    ends[1:2, :] = admittances[...]
     at_ends = folded(dot(vb[...], eg[...]))
     launch_part(size, lambda d: waves[d], ends, at_ends, kk, drive, up, down)
 
@@ -404,10 +434,11 @@
     branch, filt, amps, volt, peak, at_ends, *refs,
 ):
     if last:
-        back, branch_out = refs[:2]
-    cols, x, vb, sem = refs[-4:]
-    cols_copy = pltpu.make_async_copy(cols_hbm, cols, sem)
-    cols_copy.start()
+        back, branch_hbm, volt_hbm, peak_hbm, branch_out = *refs[:4], refs[-1]
+        refs = refs[4:-1]
+    cols, x, vb, sems = refs
+    copies = Copies(sems)
+    cols_copy = copies.start(cols_hbm, cols)
     pair = stacked(drive[...])
     for b in range(size.blocks):
         added = three_terms(dot(pair, mt[b]), size.scen, size.padded)
@@ -427,14 +458,20 @@
         branch[b] = history
         x[b] = stacked(rest_of(size, node_rows, b, history, volt[b], site, level) + injected)
     cols_copy.wait()
+    if last:
+        unpad_blocks(size, lambda b: branch[b], branch_out)
+        sent = [copies.start(branch_out, branch_hbm), copies.start(peak, peak_hbm)]
     apply_inverse(size, cols, x, wp, volt, vb)
+    if last:
+        sent.append(copies.start(volt, volt_hbm))
     at_ends[...] = folded(dot(vb[...], eg[...]))
     if last:
         for c in range(0, size.slot_lanes, LANES):
             count = min(LANES, size.slots - c)
             part = jnp.concatenate([filt[:, c : c + LANES], amps[:, c : c + LANES]], axis=0)
             back[c : c + count, :] = part.T[:count]
-        unpad_blocks(size, lambda b: branch[b], branch_out)
+        for copy in sent:
+            copy.wait()
 
 
 def launch_kernel(size, done, last, at_ends, kk, ends, waves, *refs):
@@ -449,7 +486,8 @@
         back, refs = refs[0], refs[1:]
     drive, up, down = refs[:3]
     if last:
-        chunks, waves_out, recent, sems = refs[3:]
+        drive_hbm = drive
+        chunks, waves_out, recent, drive, sems = refs[3:]
         copies = Copies(sems)
         sent = [copies.start(back, chunks)]
         for d in range(done):
@@ -459,12 +497,17 @@
         sent.append(copies.start(waves.at[pl.ds(0, kept)], waves_out.at[pl.ds(1 + done, kept)]))
     launch_part(size, history, ends, at_ends[...], kk, drive, up, down)
     if last:
+        sent.append(copies.start(drive, drive_hbm))
         for copy in sent:
             copy.wait()
 
 
-def final_kernel(size, drive, volt_hbm, mt_hbm, peak_hbm, voltage_out, peak_out, volt, mt, peak, sems):
+def final_kernel(
+    size, drive_hbm, volt_hbm, mt_hbm, peak_hbm, voltage_hbm, top_hbm,
+    drive, volt, mt, peak, voltage_out, peak_out, sems,
+):
     copies = Copies(sems)
+    drive_copy = copies.start(drive_hbm, drive)
     half = size.blocks // 2
     parts = []
     for i in range(2):
@@ -473,13 +516,13 @@
             [copies.start(volt_hbm.at[part], volt.at[part]), copies.start(mt_hbm.at[part], mt.at[part])]
         )
     peak_copy = copies.start(peak_hbm, peak)
+    drive_copy.wait()
     pair = stacked(drive[...])
     for b in range(size.blocks):
         if b % half == 0:
             for copy in parts[b // half]:
                 copy.wait()
         volt[b] = volt[b] + three_terms(dot(pair, mt[b]), size.scen, size.padded)
-    unpad_blocks(size, lambda b: volt[b], voltage_out)
     peak_copy.wait()
 
     def largest(b):
@@ -487,25 +530,37 @@
         return jnp.maximum(top, jnp.max(peak[b], axis=0, keepdims=True))
 
     unpad_blocks(size, largest, peak_out)
+    sent = [copies.start(peak_out, top_hbm)]
+    unpad_blocks(size, lambda b: volt[b], voltage_out)
+    sent.append(copies.start(voltage_out, voltage_hbm))
+    for copy in sent:
+        copy.wait()
 
 
 def end_kernel(size, peaks, dst_hbm, received_hbm, ahead, after, waves_in, *refs):
     own, refs = refs[:peaks], refs[peaks:]
-    state_out, waves_out, envelope_out, dst, received, newest, tops, sems = refs
+    (
+        state_hbm, waves_out, envelope_hbm,
+        dst, received, newest, arrived, tops, state_out, envelope_out, sems,
+    ) = refs
     copies = Copies(sems)
     received_copy = copies.start(received_hbm, received)
     dst_copy = copies.start(dst_hbm, dst)
     top_copies = [copies.start(ref, tops.at[i]) for i, ref in enumerate(own)]
     lines = size.lines
-    newest[0, :, :lines] = ahead[...]
-    newest[0, :, lines:] = after[...]
-    newest_copy = copies.start(newest, waves_out.at[pl.ds(0, 1)])
+    arrived_copies = [copies.start(ahead, arrived.at[0]), copies.start(after, arrived.at[1])]
+    for copy in arrived_copies:
+        copy.wait()
+    newest[0, :, :lines] = arrived[0]
+    newest[0, :, lines:] = arrived[1]
+    sent = [copies.start(newest, waves_out.at[pl.ds(0, 1)])]
     for copy in top_copies:
         copy.wait()
     top = tops[0]
     for i in range(1, peaks):
         top = jnp.maximum(top, tops[i])
     envelope_out[...] = top
+    sent.append(copies.start(envelope_out, envelope_hbm))
     dst_copy.wait()
     select = one_hot(iota((size.slots, size.convs), 0) == dst[...])
     received_copy.wait()
@@ -515,7 +570,9 @@
     state = state[:width] + state[width : 2 * width] + state[2 * width :]
     state_out[0] = state[: size.scen]
     state_out[1] = state[size.scen :]
-    newest_copy.wait()
+    sent.append(copies.start(state_out, state_hbm))
+    for copy in sent:
+        copy.wait()
 
 
 def shape(dims, dtype=F32):
@@ -524,6 +581,10 @@
 
 def in_vmem(*values):
     return [pltpu.with_memory_space_constraint(v, pltpu.VMEM) for v in values]
+
+
+def in_hbm(*values):
+    return [pltpu.with_memory_space_constraint(v, pltpu.HBM) for v in values]
 
 
 def call(kernel, name, outs, out_specs, args, specs, scratch, limit, aliases=None):
@@ -549,29 +610,30 @@
     ring = [(i, (i + 1) % regions) for i in range(regions)]
     back_ring = [(j, i) for i, j in ring]
     dma = pltpu.SemaphoreType.DMA
-    vmem = pltpu.VMEM
+    vmem, hbm = pltpu.VMEM, pltpu.HBM
 
     def row(vector):
         return vector.reshape(1, -1)
 
-    table = jnp.stack(
-        [
-            conv_region[:, 0].astype(F32),
-            conv_power,
-            conv_gains[0],
-            conv_gains[1],
-            conv_node.astype(F32),
-        ]
-    )
-    table = jnp.concatenate([table, jnp.zeros((3, size.convs), F32)], axis=0)
+    first_row = jnp.arange(2, dtype=I32)[:, None] == 0
+    table = jnp.where(first_row, conv_power[None, :], conv_node.astype(F32)[None, :])
+    chunk = (regions, rows, 2 * scen)
     packed, dst = call(
         functools.partial(pack_kernel, size),
         "pack",
-        [shape((regions, rows, 2 * scen)), shape((1, size.convs), I32)],
-        [VMEM] * 2,
-        [table, conv_init],
+        [hbm(chunk, F32), hbm((1, size.convs), I32)],
         [HBM] * 2,
-        [vmem(table.shape, F32), vmem(conv_init.shape, F32), dma((2,))],
+        in_hbm(row(conv_region), table, conv_gains, conv_init),
+        [HBM] * 4,
+        [
+            vmem((1, size.convs), I32),
+            vmem(table.shape, F32),
+            vmem(conv_gains.shape, F32),
+            vmem(conv_init.shape, F32),
+            vmem(chunk, F32),
+            vmem((1, size.convs), I32),
+            dma((6,)),
+        ],
         16,
     )
     received = lax.all_to_all(packed, "region", split_axis=0, concat_axis=0, tiled=True)
@@ -600,9 +662,9 @@
     wp_hbm, eg_hbm, mt_hbm, kk_hbm, vb_hbm, branch_hbm, rest_hbm, rows_hbm, fault_hbm = call(
         functools.partial(prep_kernel, size),
         "prep",
-        [shape(*item) for item in kept],
+        [hbm(*item) for item in kept],
         [HBM] * len(kept),
-        args,
+        in_hbm(*args),
         [HBM] * len(args),
         [
             cols_scratch,
@@ -652,7 +714,7 @@
         shape(size.exchange),
     ]
     args = [
-        cols, received, wave_init, row(line_delay.astype(F32)), row(line_admittance), wp_hbm, eg_hbm,
+        cols, received, wave_init, row(line_delay), row(line_admittance), wp_hbm, eg_hbm,
         mt_hbm, kk_hbm, vb_hbm, branch_hbm, rest_hbm, rows_hbm, fault_hbm,
     ]
     (
@@ -663,12 +725,13 @@
         "start",
         outs,
         [VMEM] * len(outs),
-        args,
+        in_hbm(*args),
         [HBM] * len(args),
         [
             cols_scratch,
             vmem((size.slots, 2 * scen), F32),
-            vmem((2, 1, size.ends), F32),
+            vmem((1, size.ends), I32),
+            vmem((1, size.ends), F32),
             vmem(size.state, F32),
             x_scratch,
             wide_scratch,
@@ -690,19 +753,28 @@
             vmem(size.node_rows, F32),
             vmem(size.drive, F32),
         ]
+        specs = [VMEM] * len(outs)
+        scratch = [cols_scratch, x_scratch, wide_scratch, dma((4,))]
         if last:
-            outs += [vmem((size.slots, 2 * scen), F32), shape((scen, size.nodes))]
+            outs += [
+                vmem((size.slots, 2 * scen), F32),
+                hbm((scen, size.nodes), F32),
+                hbm(size.state, F32),
+                hbm(size.node_rows, F32),
+            ]
+            specs += [VMEM, HBM, HBM, HBM]
+            scratch.append(vmem((scen, size.nodes), F32))
         result = call(
             functools.partial(middle_kernel, size, last),
             "middle",
             outs,
-            [VMEM] * len(outs),
-            [cols]
+            specs,
+            in_hbm(cols)
             + in_vmem(
                 drive, wp, eg, mt, node_rows, fault_cols, cg, cs, prm, branch, filt, amps, volt, peak
             ),
             [HBM] + [VMEM] * 14,
-            [cols_scratch, x_scratch, wide_scratch, dma],
+            scratch,
             8,
             {10: 0, 11: 1, 12: 2, 13: 3, 14: 4},
         )
@@ -712,12 +784,13 @@
         outs = [vmem(size.drive, F32), shape(size.exchange), shape(size.exchange)]
         specs, scratch = [VMEM] * 3, []
         if last:
-            back, branch_out = result[6:]
+            back, branch_out, volt, peak = result[6:]
             args += in_vmem(back)
-            outs[0] = shape(size.drive)
-            outs += [shape((size.slots, 2 * scen)), shape(wave_init.shape)]
+            outs[0] = hbm(size.drive, F32)
+            outs += [hbm((size.slots, 2 * scen), F32), hbm(wave_init.shape, F32)]
+            specs[0] = HBM
             specs += [HBM, HBM]
-            scratch = [vmem((step, *size.drive), F32), dma((3,))]
+            scratch = [vmem((step, *size.drive), F32), vmem(size.drive, F32), dma((4,))]
         drive, up, down, *rest = call(
             functools.partial(launch_kernel, size, step, last),
             "launch",
@@ -736,15 +809,18 @@
     voltage_out, peak_out = call(
         functools.partial(final_kernel, size),
         "final",
-        [shape((scen, size.nodes)), shape((1, size.nodes))],
-        [VMEM] * 2,
-        [drive, volt, mt_hbm, peak],
-        [VMEM, HBM, HBM, HBM],
+        [hbm((scen, size.nodes), F32), hbm((1, size.nodes), F32)],
+        [HBM] * 2,
+        in_hbm(drive, volt, mt_hbm, peak),
+        [HBM] * 4,
         [
+            vmem(size.drive, F32),
             vmem(size.state, F32),
             vmem(size.response, BF),
             vmem(size.node_rows, F32),
-            dma((5,)),
+            vmem((scen, size.nodes), F32),
+            vmem((1, size.nodes), F32),
+            dma((8,)),
         ],
         12,
     )
@@ -758,16 +834,19 @@
     conv_state, wave_history, envelope = call(
         functools.partial(end_kernel, size, len(peaks)),
         "end",
-        [shape(conv_init.shape), shape(wave_init.shape), shape((1, size.nodes))],
-        [VMEM, HBM, VMEM],
-        args,
-        [HBM, HBM, VMEM, VMEM] + [HBM] * (len(args) - 4),
+        [hbm(conv_init.shape, F32), hbm(wave_init.shape, F32), hbm((1, size.nodes), F32)],
+        [HBM] * 3,
+        in_hbm(*args),
+        [HBM] * len(args),
         [
             vmem(dst.shape, I32),
             vmem(returned.shape, F32),
             vmem((1, *size.drive), F32),
+            vmem((2, *size.exchange), F32),
             vmem((others, 1, size.nodes), F32),
-            dma((3 + others,)),
+            vmem(conv_init.shape, F32),
+            vmem((1, size.nodes), F32),
+            dma((7 + others,)),
         ],
         16,
         {4: 1},

time: 130 us -> 106 us (0.82)
  local copies, waits for them, and re-layouts: 30.6 us -> 1.57 us
  Pallas kernels: 60.7 us -> 65.7 us
    unnamed x52 -> x14, local copies, waits for them, and re-layouts: 29.2 us -> 1.57 us
    pallas_call x11, Pallas kernels: 60.7 us -> 65.7 us  [call(): pl.pallas_call(kernel, name=name, out_shape=outs, in_specs=specs, out_spe...]
    convert_element_type x3 -> x1, other arithmetic: 2.1 us -> 0.69 us  [shards(): conv_node.astype(F32)[None, :]]
    select_n x0 -> x1, other arithmetic: none -> 1.33 us  [shards(): jnp.where(first_row, conv_power[None, :], conv_node.astype(F32)[None, :])]
  transfers between devices with their start and end apart: 13 -> 13, of which waited for: 2 -> 2; matrix products, arithmetic and copies ran while one was open for 1% -> 0% of each run, Pallas kernels for 32% -> 44%
where the time goes in v2:
time: 106 us; the launch traced here: 105 us
  Pallas kernels  65.7 us (62%)
  starting transfers between devices  31.9 us (30%)
  waiting for transfers between devices  3.19 us (3%)
  other arithmetic  2.02 us (2%)
  local copies, waits for them, and re-layouts  1.57 us (1%)
    pallas_call x11, Pallas kernels, call(): pl.pallas_call(kernel, name=name, out_shape=outs, in_specs=specs, out_spe...  65.7 us
    ppermute x4, starting transfers between devices, shards(): from_after = lax.ppermute(down, 'region', back_ring)  15.2 us
    all_to_all x1, starting transfers between devices, shards(): lax.all_to_all(packed, 'region', split_axis=0, concat_axis=0, tiled=True)  7.29 us
    ppermute x4, starting transfers between devices, shards(): from_ahead = lax.ppermute(up, 'region', ring)  4.11 us
    all_to_all x1, starting transfers between devices, shards(): lax.all_to_all(chunks, 'region', split_axis=0, concat_axis=0, tiled=True)  3.49 us
    ppermute x3, waiting for transfers between devices, shards(): lax.ppermute(peak_out, 'scen', [(i, (i + d) % others) for i in range(othe...  3.16 us
  transfers between devices with their start and end apart: 13, of which 2 were waited for; matrix products, arithmetic and copies ran while one was open for 0% of the time, Pallas kernels for 44%

profile of v2, /device:TPU:0, one launch (start us, length us, event | category | flops | bytes accessed | tf_op | source)
XLA Modules:
  0.0 105.4 jit_solution(4374074594501990591)
XLA Ops:
  0.6 0.7 convert_element_type.3
  1.3 1.3 %broadcast_select_fusion.table_hbm = f32[2,384]{1,0:T(2,128)} fusion(pred[2]{0:T(512)(128)(4,1)S(1)} %iota_compare_fusion, f32[384]{0:T(512)S(1)} %convert_element_type.3, f32[384]{0:T(512)} %param.31), kind=kLoop, calls=%fused_computation | loop fusion | flops 768 | bytes 6146 | tf_op jit(solution)/shard_map/jit(_where)/select_n | solution.py:619
  2.7 3.0 %pack.1 = (f32[8,120,128]{2,1,0:T(8,128)}, s32[1,384]{1,0:T(1,128)}) custom-call(s32[1,384]{1,0:T(1,128)} %bitcast.25, f32[2,384]{1,0:T(2,128)} %broadcast_select_fusion.table_hbm, f32[2,384]{1,0:T(2,128)} %gains_hbm.1, f32[2,64,384]{2,1,0:T(8,128)} %init_hbm.1), custom_call_target="tpu_custom_call" | custom-call | tf_op jit(solution)/shard_map/pack/pallas_call | solution.py:591
  5.7 7.3 %all-to-all-start = ((f32[8,120,128]{2,1,0:T(8,128)}), f32[8,120,128]{2,1,0:T(8,128)S(1)}, u32[]{:S(2)}, u32[]{:S(2)}) async-start(f32[8,120,128]{2,1,0:T(8,128)} %get-tuple-element.68), calls=%async_computation | async-start | bytes 983040 | tf_op jit(solution)/shard_map/all_to_all | solution.py:639
  13.0 15.3 %prep.1 = (bf16[32,480,256]{2,1,0:T(8,128)(2,1)}, bf16[4096,256]{1,0:T(8,128)(2,1)}, bf16[32,256,256]{2,1,0:T(8,128)(2,1)}, bf16[256,512]{1,0:T(8,128)(2,1)}, bf...) custom-call(s32[5,32]{1,0:T(8,128)} %bitcast.17, ...), custom_call_target="tpu_custom_call" | custom-call | tf_op jit(solution)/shard_map/prep/pallas_call | solution.py:591
  28.3 0.8 copy-done.1
  29.0 12.5 %start.1 = (bf16[32,480,256]{2,1,0:T(8,128)(2,1)S(1)}, bf16[4096,256]{1,0:T(8,128)(2,1)S(1)}, bf16[32,256,256]{2,1,0:T(8,128)(2,1)S(1)}, bf16[256,512]{1,0:T(8,1...) custom-call(s32[5,32]{1,0:T(8,128)} %bitcast.18, ...), custom_call_target="tpu_custom_call" | custom-call | tf_op jit(solution)/shard_map/start/pallas_call | solution.py:591
  41.5 2.1 %collective-permute-start = (f32[64,128]{1,0:T(8,128)S(1)}, f32[64,128]{1,0:T(8,128)S(1)}, u32[]{:S(2)}, u32[]{:S(2)}) collective-permute-start(f32[64,128]{1,0:T(8,128)S(1)} %get-tuple-element.96), channel_id=1, source_target_pairs={{0,4},{4,8},{8,12},{12,16},{16,20},{20,24},{24,28},{28,0},{1,5},{5... | collective-permute-start | bytes 98312 | tf_op jit(solution)/shard_map/ppermute | solution.py:746
  43.6 2.9 %collective-permute-start.1 = (f32[64,128]{1,0:T(8,128)S(1)}, f32[64,128]{1,0:T(8,128)S(1)}, u32[]{:S(2)}, u32[]{:S(2)}) collective-permute-start(f32[64,128]{1,0:T(8,128)S(1)} %get-tuple-element.97), channel_id=1, source_target_pairs={{4,0},{8,4},{12,8},{16,12},{20,16},{24,20},{28,24},{0,28},{5,1},{9... | collective-permute-start | bytes 98312 | tf_op jit(solution)/shard_map/ppermute | solution.py:747
  46.6 8.6 %middle.3 = (f32[32,64,128]{2,1,0:T(8,128)S(1)}, f32[64,1024]{1,0:T(8,128)S(1)}, f32[64,1024]{1,0:T(8,128)S(1)}, f32[32,64,128]{2,1,0:T(8,128)S(1)}, f32[32,8,128]{2,1,0:T(8,128)S(1)}, /*index=5*/f32[64,256]{1,0:T(8,128)S(1)}) custom-call(s32[5,32]{1,0:T(8,128)} %bitcast.19, ...), custom_call_target="tpu_custom_call", output_to_operand_aliasing={{0}: (10, {}), {1}: (11, {}), {2}: (12, {}), {3}: (13, {}),... | custom-call | tf_op jit(solution)/shard_map/middle/pallas_call | solution.py:591
  55.2 0.2 launch.3
  55.4 0.1 collective-permute-start.2
  55.5 4.7 %collective-permute-start.3 = (f32[64,128]{1,0:T(8,128)S(1)}, f32[64,128]{1,0:T(8,128)S(1)}, u32[]{:S(2)}, u32[]{:S(2)}) collective-permute-start(f32[64,128]{1,0:T(8,128)S(1)} %get-tuple-element.106), channel_id=1, source_target_pairs={{4,0},{8,4},{12,8},{16,12},{20,16},{24,20},{28,24},{0,28},{5,1},{9... | collective-permute-start | bytes 98312 | tf_op jit(solution)/shard_map/ppermute | solution.py:747
  60.2 8.6 %middle.4 = (f32[32,64,128]{2,1,0:T(8,128)S(1)}, f32[64,1024]{1,0:T(8,128)S(1)}, f32[64,1024]{1,0:T(8,128)S(1)}, f32[32,64,128]{2,1,0:T(8,128)S(1)}, f32[32,8,128]{2,1,0:T(8,128)S(1)}, /*index=5*/f32[64,256]{1,0:T(8,128)S(1)}) custom-call(s32[5,32]{1,0:T(8,128)} %bitcast.20, ...), custom_call_target="tpu_custom_call", output_to_operand_aliasing={{0}: (10, {}), {1}: (11, {}), {2}: (12, {}), {3}: (13, {}),... | custom-call | tf_op jit(solution)/shard_map/middle/pallas_call | solution.py:591
  68.9 0.2 launch.4
  69.1 0.1 collective-permute-start.4
  69.1 4.7 %collective-permute-start.5 = (f32[64,128]{1,0:T(8,128)S(1)}, f32[64,128]{1,0:T(8,128)S(1)}, u32[]{:S(2)}, u32[]{:S(2)}) collective-permute-start(f32[64,128]{1,0:T(8,128)S(1)} %get-tuple-element.115), channel_id=1, source_target_pairs={{4,0},{8,4},{12,8},{16,12},{20,16},{24,20},{28,24},{0,28},{5,1},{9... | collective-permute-start | bytes 98312 | tf_op jit(solution)/shard_map/ppermute | solution.py:747
  73.8 9.4 %middle.5 = (f32[32,64,128]{2,1,0:T(8,128)S(1)}, f32[64,1024]{1,0:T(8,128)S(1)}, f32[64,1024]{1,0:T(8,128)S(1)}, f32[32,64,128]{2,1,0:T(8,128)S(1)}, f32[32,8,12...) custom-call(s32[5,32]{1,0:T(8,128)} %bitcast.21, ...), custom_call_target="tpu_custom_call", output_to_operand_aliasing={{0}: (10, {}), {1}: (11, {}), {2}: (12, {}), {3}: (13, {}),... | custom-call | tf_op jit(solution)/shard_map/middle/pallas_call | solution.py:591
  83.2 1.0 launch.5
  84.2 3.5 %all-to-all-start.1 = ((f32[8,120,128]{2,1,0:T(8,128)}), f32[8,120,128]{2,1,0:T(8,128)S(1)}, u32[]{:S(2)}, u32[]{:S(2)}) async-start(f32[8,120,128]{2,1,0:T(8,128)} %bitcast.16), calls=%async_computation.1 | async-start | bytes 983040 | tf_op jit(solution)/shard_map/all_to_all | solution.py:808
  87.7 1.9 %collective-permute-start.6 = (f32[64,128]{1,0:T(8,128)S(1)}, f32[64,128]{1,0:T(8,128)S(1)}, u32[]{:S(2)}, u32[]{:S(2)}) collective-permute-start(f32[64,128]{1,0:T(8,128)S(1)} %get-tuple-element.124), channel_id=1, source_target_pairs={{0,4},{4,8},{8,12},{12,16},{16,20},{20,24},{24,28},{28,0},{1,5},{5... | collective-permute-start | bytes 98312 | tf_op jit(solution)/shard_map/ppermute | solution.py:805
  89.7 2.9 %collective-permute-start.7 = (f32[64,128]{1,0:T(8,128)S(1)}, f32[64,128]{1,0:T(8,128)S(1)}, u32[]{:S(2)}, u32[]{:S(2)}) collective-permute-start(f32[64,128]{1,0:T(8,128)S(1)} %get-tuple-element.125), channel_id=1, source_target_pairs={{4,0},{8,4},{12,8},{16,12},{20,16},{24,20},{28,24},{0,28},{5,1},{9... | collective-permute-start | bytes 98312 | tf_op jit(solution)/shard_map/ppermute | solution.py:806
  92.5 4.3 %final.1 = (f32[64,3072]{1,0:T(8,128)}, f32[1,3072]{1,0:T(1,128)}) custom-call(f32[64,256]{1,0:T(8,128)} %get-tuple-element.117.drive_hbm, f32[32,64,128]{2,1,0:T(8,128)} %get-tuple-element.118.volt_hbm, bf16[32,256,256]{2,1,0:T(8,128)(2,1)} %get-tuple-element.71.mt_hbm, f32[32,8,128]{2,1,0:T(8,128)} %get-tuple-element.119.peak_hbm), custom_call_target="tpu_custom_call" | custom-call | tf_op jit(solution)/shard_map/final/pallas_call | solution.py:591
  96.8 0.1 collective-permute-start.10
  96.9 1.6 %collective-permute-start.9 = (f32[1,3072]{1,0:T(1,128)}, f32[1,3072]{1,0:T(1,128)S(1)}, u32[]{:S(2)}, u32[]{:S(2)}) collective-permute-start(f32[1,3072]{1,0:T(1,128)} %get-tuple-element.127.refs_0_), channel_id=1, source_target_pairs={{0,2},{1,3},{2,0},{3,1},{4,6},{5,7},{6,4},{7,5},{8,10},{9,11},{10,... | collective-permute-start | bytes 36872 | tf_op jit(solution)/shard_map/ppermute | solution.py:829
  98.5 0.2 collective-permute-start.8
  98.6 2.2 %collective-permute-done.9.refs_2_ = f32[1,3072]{1,0:T(1,128)S(1)} collective-permute-done((f32[1,3072]{1,0:T(1,128)}, f32[1,3072]{1,0:T(1,128)S(1)}, u32[]{:S(2)}, u32[]{:S(2)}) %collective-permute-start.9) | collective-permute-done | bytes 12320 | tf_op jit(solution)/shard_map/ppermute | solution.py:829
  100.9 0.9 collective-permute-done.8.refs_1_
  101.8 0.5 copy-done.6
  102.4 0.0 copy-done.2
  102.4 0.2 copy-done
  102.6 2.6 %end.1 = (f32[2,64,384]{2,1,0:T(8,128)}, f32[8,64,256]{2,1,0:T(8,128)}, f32[1,3072]{1,0:T(1,128)}) custom-call(s32[1,384]{1,0:T(1,128)} %get-tuple-element.122.dst_hbm, f32[960,128]{1,0:T(8,128)} %bitcast.14, f32[64,128]{1,0:T(8,128)} %copy-done.2, f32[64,128]{1,0:T(8,128)} %copy-done.3, ...), custom_call_target="tpu_custom_call", output_to_operand_aliasing={{1}: (4, {})} | custom-call | tf_op jit(solution)/shard_map/end/pallas_call | solution.py:591
  (22 shorter events, 0.1 us)
Async XLA Ops:
  5.7 22.6 %all-to-all-start = ((f32[8,120,128]{2,1,0:T(8,128)}), f32[8,120,128]{2,1,0:T(8,128)S(1)}, u32[]{:S(2)}, u32[]{:S(2)}) async-start(f32[8,120,128]{2,1,0:T(8,128)} %get-tuple-element.68), calls=%async_computation | async-start | bytes 983040 | tf_op jit(solution)/shard_map/all_to_all | solution.py:639
  28.3 0.8 copy-start.1
  41.5 13.7 %collective-permute-start = (f32[64,128]{1,0:T(8,128)S(1)}, f32[64,128]{1,0:T(8,128)S(1)}, u32[]{:S(2)}, u32[]{:S(2)}) collective-permute-start(f32[64,128]{1,0:T(8,128)S(1)} %get-tuple-element.96), channel_id=1, source_target_pairs={{0,4},{4,8},{8,12},{12,16},{16,20},{20,24},{24,28},{28,0},{1,5},{5... | collective-permute-start | bytes 98312 | tf_op jit(solution)/shard_map/ppermute | solution.py:746
  43.6 11.6 %collective-permute-start.1 = (f32[64,128]{1,0:T(8,128)S(1)}, f32[64,128]{1,0:T(8,128)S(1)}, u32[]{:S(2)}, u32[]{:S(2)}) collective-permute-start(f32[64,128]{1,0:T(8,128)S(1)} %get-tuple-element.97), channel_id=1, source_target_pairs={{4,0},{8,4},{12,8},{16,12},{20,16},{24,20},{28,24},{0,28},{5,1},{9... | collective-permute-start | bytes 98312 | tf_op jit(solution)/shard_map/ppermute | solution.py:747
  55.4 13.4 %collective-permute-start.2 = (f32[64,128]{1,0:T(8,128)S(1)}, f32[64,128]{1,0:T(8,128)S(1)}, u32[]{:S(2)}, u32[]{:S(2)}) collective-permute-start(f32[64,128]{1,0:T(8,128)S(1)} %get-tuple-element.105), channel_id=1, source_target_pairs={{0,4},{4,8},{8,12},{12,16},{16,20},{20,24},{24,28},{28,0},{1,5},{5... | collective-permute-start | bytes 98312 | tf_op jit(solution)/shard_map/ppermute | solution.py:746
  55.5 13.4 %collective-permute-start.3 = (f32[64,128]{1,0:T(8,128)S(1)}, f32[64,128]{1,0:T(8,128)S(1)}, u32[]{:S(2)}, u32[]{:S(2)}) collective-permute-start(f32[64,128]{1,0:T(8,128)S(1)} %get-tuple-element.106), channel_id=1, source_target_pairs={{4,0},{8,4},{12,8},{16,12},{20,16},{24,20},{28,24},{0,28},{5,1},{9... | collective-permute-start | bytes 98312 | tf_op jit(solution)/shard_map/ppermute | solution.py:747
  69.1 14.2 %collective-permute-start.4 = (f32[64,128]{1,0:T(8,128)S(1)}, f32[64,128]{1,0:T(8,128)S(1)}, u32[]{:S(2)}, u32[]{:S(2)}) collective-permute-start(f32[64,128]{1,0:T(8,128)S(1)} %get-tuple-element.114), channel_id=1, source_target_pairs={{0,4},{4,8},{8,12},{12,16},{16,20},{20,24},{24,28},{28,0},{1,5},{5... | collective-permute-start | bytes 98312 | tf_op jit(solution)/shard_map/ppermute | solution.py:746
  69.1 14.1 %collective-permute-start.5 = (f32[64,128]{1,0:T(8,128)S(1)}, f32[64,128]{1,0:T(8,128)S(1)}, u32[]{:S(2)}, u32[]{:S(2)}) collective-permute-start(f32[64,128]{1,0:T(8,128)S(1)} %get-tuple-element.115), channel_id=1, source_target_pairs={{4,0},{8,4},{12,8},{16,12},{20,16},{24,20},{28,24},{0,28},{5,1},{9... | collective-permute-start | bytes 98312 | tf_op jit(solution)/shard_map/ppermute | solution.py:747
  84.2 17.6 %all-to-all-start.1 = ((f32[8,120,128]{2,1,0:T(8,128)}), f32[8,120,128]{2,1,0:T(8,128)S(1)}, u32[]{:S(2)}, u32[]{:S(2)}) async-start(f32[8,120,128]{2,1,0:T(8,128)} %bitcast.16), calls=%async_computation.1 | async-start | bytes 983040 | tf_op jit(solution)/shard_map/all_to_all | solution.py:808
  87.7 14.1 %collective-permute-start.6 = (f32[64,128]{1,0:T(8,128)S(1)}, f32[64,128]{1,0:T(8,128)S(1)}, u32[]{:S(2)}, u32[]{:S(2)}) collective-permute-start(f32[64,128]{1,0:T(8,128)S(1)} %get-tuple-element.124), channel_id=1, source_target_pairs={{0,4},{4,8},{8,12},{12,16},{16,20},{20,24},{24,28},{28,0},{1,5},{5... | collective-permute-start | bytes 98312 | tf_op jit(solution)/shard_map/ppermute | solution.py:805
  89.7 12.1 %collective-permute-start.7 = (f32[64,128]{1,0:T(8,128)S(1)}, f32[64,128]{1,0:T(8,128)S(1)}, u32[]{:S(2)}, u32[]{:S(2)}) collective-permute-start(f32[64,128]{1,0:T(8,128)S(1)} %get-tuple-element.125), channel_id=1, source_target_pairs={{4,0},{8,4},{12,8},{16,12},{20,16},{24,20},{28,24},{0,28},{5,1},{9... | collective-permute-start | bytes 98312 | tf_op jit(solution)/shard_map/ppermute | solution.py:806
  96.8 1.8 %collective-permute-start.10 = (f32[1,3072]{1,0:T(1,128)}, f32[1,3072]{1,0:T(1,128)S(1)}, u32[]{:S(2)}, u32[]{:S(2)}) collective-permute-start(f32[1,3072]{1,0:T(1,128)} %get-tuple-element.127.refs_0_), channel_id=1, source_target_pairs={{0,3},{1,0},{2,1},{3,2},{4,7},{5,4},{6,5},{7,6},{8,11},{9,8},{10,9... | collective-permute-start | bytes 36872 | tf_op jit(solution)/shard_map/ppermute | solution.py:829
  96.9 4.0 %collective-permute-start.9 = (f32[1,3072]{1,0:T(1,128)}, f32[1,3072]{1,0:T(1,128)S(1)}, u32[]{:S(2)}, u32[]{:S(2)}) collective-permute-start(f32[1,3072]{1,0:T(1,128)} %get-tuple-element.127.refs_0_), channel_id=1, source_target_pairs={{0,2},{1,3},{2,0},{3,1},{4,6},{5,7},{6,4},{7,5},{8,10},{9,11},{10,... | collective-permute-start | bytes 36872 | tf_op jit(solution)/shard_map/ppermute | solution.py:829
  98.5 3.3 %collective-permute-start.8 = (f32[1,3072]{1,0:T(1,128)}, f32[1,3072]{1,0:T(1,128)S(1)}, u32[]{:S(2)}, u32[]{:S(2)}) collective-permute-start(f32[1,3072]{1,0:T(1,128)} %get-tuple-element.127.refs_0_), channel_id=1, source_target_pairs={{0,1},{1,2},{2,3},{3,0},{4,5},{5,6},{6,7},{7,4},{8,9},{9,10},{10,1... | collective-permute-start | bytes 36872 | tf_op jit(solution)/shard_map/ppermute | solution.py:829
  98.6 3.2 %copy-start.4 = (f32[1,3072]{1,0:T(1,128)}, f32[1,3072]{1,0:T(1,128)S(1)}, u32[]{:S(2)}) copy-start(f32[1,3072]{1,0:T(1,128)S(1)} %collective-permute-done.10.refs_3_) | copy-start | bytes 36868
  100.9 1.0 copy-start.5
  101.8 0.6 copy-start.6
  101.8 0.6 copy-start.2
  101.8 0.6 copy-start.3
  101.8 0.8 copy-start

commit v3 on v2

--- a/solution.py
+++ b/solution.py
@@ -126,14 +126,18 @@
 
 
 def pack_kernel(
-    size, region_hbm, table_hbm, gains_hbm, init_hbm, out_hbm, dst_hbm,
-    region, table, gains, init, out, dst_out, sems,
+    size, region_hbm, power_hbm, node_hbm, gains_hbm, init_hbm, out_hbm, dst_hbm,
+    region, power, node, gains, init, out, dst_out, sems,
 ):
     convs, slots = size.convs, size.slots
     copies = Copies(sems)
     first = copies.start(region_hbm, region)
     second = copies.start(init_hbm, init)
-    others = [copies.start(table_hbm, table), copies.start(gains_hbm, gains)]
+    others = [
+        copies.start(power_hbm, power),
+        copies.start(node_hbm, node),
+        copies.start(gains_hbm, gains),
+    ]
     first.wait()
     target = region[...]
     member = iota((round_up(size.regions, 16), convs), 0) == target
@@ -146,9 +150,13 @@
     sent = [copies.start(dst_out, dst_hbm)]
     for copy in others:
         copy.wait()
-    settings = jnp.concatenate(
-        [table[0:1, :], gains[...], table[1:2, :], jnp.zeros((LANES - 4, convs), F32)], axis=0
-    )
+    rows = [
+        power[...].reshape(1, convs),
+        gains[...],
+        node[...].astype(F32).reshape(1, convs),
+        jnp.zeros((LANES - 4, convs), F32),
+    ]
+    settings = jnp.concatenate(rows, axis=0)
     second.wait()
     state = jnp.concatenate([init[0], init[1]], axis=0)
     payload = jnp.concatenate([state.T, settings.T], axis=1)
@@ -293,33 +301,32 @@
     sent.append(copies.start(rest, rest_out))
 
     cols_copy.wait()
+    zeros = jnp.zeros((size.width, size.padded - size.width), BF)
+    zero_rows = jnp.zeros((size.padded - size.width, 2 * size.padded), BF)
     for i, copy in enumerate(weight_copies):
         copy.wait()
 
         def turn(b, carry):
+            parts = []
             for k in range(size.picks):
                 high, low = split_2(raw[b, k].T)
-                zeros = jnp.zeros((size.width, size.padded - size.width), BF)
-                wp[b, k * size.width : (k + 1) * size.width, :] = jnp.concatenate(
-                    [high, zeros, low, zeros], axis=1
-                )
+                part = jnp.concatenate([high, zeros, low, zeros], axis=1)
+                wp[b, k * size.width : (k + 1) * size.width, :] = part
+                parts += [part, zero_rows]
+            left = jnp.concatenate([es[cols[k, b]] for k in range(size.picks)], axis=1)
+            product = dot(left, jnp.concatenate(parts, axis=0))
+            high, low = split_2(product[:, : size.padded] + product[:, size.padded :])
+            mt[b] = jnp.concatenate([high, low], axis=1)
+            both[:, pl.ds(pl.multiple_of(b * size.padded, LANES), size.padded)] = jnp.concatenate(
+                [high, low], axis=0
+            )
             return carry
 
-        lax.fori_loop(i * stage, (i + 1) * stage, turn, 0, unroll=2)
+        lax.fori_loop(i * stage, (i + 1) * stage, turn, 0, unroll=4)
         part = pl.ds(i * stage, stage)
         sent.append(copies.start(wp.at[part], wp_out.at[part]))
-
-    def respond(b, carry):
-        product = picked_product(size, cols, b, es, wp)
-        high, low = split_2(product[:, : size.padded] + product[:, size.padded :])
-        mt[b] = jnp.concatenate([high, low], axis=1)
-        both[:, pl.ds(pl.multiple_of(b * size.padded, LANES), size.padded)] = jnp.concatenate(
-            [high, low], axis=0
-        )
-        return carry
-
-    lax.fori_loop(0, size.blocks, respond, 0, unroll=4)
-    sent.append(copies.start(mt, mt_out))
+        sent.append(copies.start(mt.at[part], mt_out.at[part]))
+
     high, low = split_2(folded(dot(both[...], eg[...])))
     kk[...] = jnp.concatenate([high, low], axis=1)
     sent.append(copies.start(kk, kk_out))
@@ -331,6 +338,15 @@
     lane = iota((size.scen, size.padded), 1).astype(F32)
     hit = jnp.where(lane + float(b * size.padded) == site, level, 0.0)
     return node_rows[b, 0:1, :] - history - hit * v
+
+
+def injections(size, pair, cs):
+    step = 2 if size.blocks % 2 == 0 else 1
+    for first in range(0, size.blocks, step):
+        lanes = slice(first * size.padded, (first + step) * size.padded)
+        both = folded(dot(pair, cs[:, lanes]))
+        for j in range(step):
+            yield first + j, both[:, block_lanes(size, j)]
 
 
 def converter_update(size, vb, cg, prm, filt, amps):
@@ -358,14 +374,13 @@
 
 def start_kernel(
     size,
-    cols_hbm, received_hbm, waves_hbm, delay_hbm, admittance_hbm,
+    cols_hbm, received, waves_hbm, delay_hbm, admittance_hbm,
     wp_hbm, eg_hbm, mt_hbm, kk_hbm, vb_hbm, branch_hbm, rest_hbm, rows_hbm, fault_hbm,
     wp, eg, mt, kk, waves, ends, node_rows, fault_cols, branch, cg, cs, prm, filt, amps, volt,
     peak, drive, up, down,
-    cols, received, delays, admittances, rest, x, vb, sems,
+    cols, delays, admittances, rest, x, vb, sems,
 ):
     copies = Copies(sems)
-    received_copy = copies.start(received_hbm, received)
     vb_copy = copies.start(vb_hbm, vb)
     rest_copy = copies.start(rest_hbm, rest)
     cols_copy = copies.start(cols_hbm, cols)
@@ -382,7 +397,6 @@
         copies.start(fault_hbm, fault_cols),
     ]
     rows, capacity, slots, regions = size.rows, size.capacity, size.slots, size.regions
-    received_copy.wait()
     settings = [
         received[r * rows + capacity : r * rows + capacity + 4, :rows] for r in range(regions)
     ]
@@ -413,8 +427,7 @@
     vb_copy.wait()
     pair = converter_update(size, vb, cg, prm, filt, amps)
     rest_copy.wait()
-    for b in range(size.blocks):
-        injected = folded(dot(pair, cs[:, block_lanes(size, b)]))
+    for b, injected in injections(size, pair, cs):
         x[b] = stacked(rest[b] + injected)
     cols_copy.wait()
     wp_copy.wait()
@@ -452,8 +465,7 @@
         peak[b] = jnp.maximum(peak[b], top)
     pair = converter_update(size, vb, cg, prm, filt, amps)
     site, level = fault_cols[0], fault_cols[1]
-    for b in range(size.blocks):
-        injected = folded(dot(pair, cs[:, block_lanes(size, b)]))
+    for b, injected in injections(size, pair, cs):
         history = node_rows[b, 1:2, :] * branch[b] + node_rows[b, 2:3, :] * volt[b]
         branch[b] = history
         x[b] = stacked(rest_of(size, node_rows, b, history, volt[b], site, level) + injected)
@@ -537,34 +549,18 @@
         copy.wait()
 
 
-def end_kernel(size, peaks, dst_hbm, received_hbm, ahead, after, waves_in, *refs):
-    own, refs = refs[:peaks], refs[peaks:]
-    (
-        state_hbm, waves_out, envelope_hbm,
-        dst, received, newest, arrived, tops, state_out, envelope_out, sems,
-    ) = refs
+def end_kernel(
+    size, dst_hbm, received, ahead, after, waves_in, state_hbm, waves_out,
+    dst, newest, state_out, sems,
+):
     copies = Copies(sems)
-    received_copy = copies.start(received_hbm, received)
     dst_copy = copies.start(dst_hbm, dst)
-    top_copies = [copies.start(ref, tops.at[i]) for i, ref in enumerate(own)]
-    lines = size.lines
-    arrived_copies = [copies.start(ahead, arrived.at[0]), copies.start(after, arrived.at[1])]
-    for copy in arrived_copies:
-        copy.wait()
-    newest[0, :, :lines] = arrived[0]
-    newest[0, :, lines:] = arrived[1]
+    newest[0, :, : size.lines] = ahead[...]
+    newest[0, :, size.lines :] = after[...]
     sent = [copies.start(newest, waves_out.at[pl.ds(0, 1)])]
-    for copy in top_copies:
-        copy.wait()
-    top = tops[0]
-    for i in range(1, peaks):
-        top = jnp.maximum(top, tops[i])
-    envelope_out[...] = top
-    sent.append(copies.start(envelope_out, envelope_hbm))
+    parts = jnp.concatenate(split_3(received[...].T), axis=0)
     dst_copy.wait()
     select = one_hot(iota((size.slots, size.convs), 0) == dst[...])
-    received_copy.wait()
-    parts = jnp.concatenate(split_3(received[...].T), axis=0)
     state = dot(parts, select)
     width = 2 * size.scen
     state = state[:width] + state[width : 2 * width] + state[2 * width :]
@@ -615,24 +611,23 @@
     def row(vector):
         return vector.reshape(1, -1)
 
-    first_row = jnp.arange(2, dtype=I32)[:, None] == 0
-    table = jnp.where(first_row, conv_power[None, :], conv_node.astype(F32)[None, :])
     chunk = (regions, rows, 2 * scen)
     packed, dst = call(
         functools.partial(pack_kernel, size),
         "pack",
         [hbm(chunk, F32), hbm((1, size.convs), I32)],
         [HBM] * 2,
-        in_hbm(row(conv_region), table, conv_gains, conv_init),
-        [HBM] * 4,
+        in_hbm(row(conv_region), conv_power, conv_node, conv_gains, conv_init),
+        [HBM] * 5,
         [
             vmem((1, size.convs), I32),
-            vmem(table.shape, F32),
+            vmem(conv_power.shape, F32),
+            vmem(conv_node.shape, I32),
             vmem(conv_gains.shape, F32),
             vmem(conv_init.shape, F32),
             vmem(chunk, F32),
             vmem((1, size.convs), I32),
-            dma((6,)),
+            dma((8,)),
         ],
         16,
     )
@@ -725,11 +720,10 @@
         "start",
         outs,
         [VMEM] * len(outs),
-        in_hbm(*args),
-        [HBM] * len(args),
+        in_hbm(cols) + in_vmem(received) + in_hbm(*args[2:]),
+        [HBM, VMEM] + [HBM] * (len(args) - 2),
         [
             cols_scratch,
-            vmem((size.slots, 2 * scen), F32),
             vmem((1, size.ends), I32),
             vmem((1, size.ends), F32),
             vmem(size.state, F32),
@@ -825,32 +819,30 @@
         12,
     )
     others = lax.axis_size("scen")
-    peaks = [peak_out] + [
-        lax.ppermute(peak_out, "scen", [(i, (i + d) % others) for i in range(others)])
-        for d in range(1, others)
-    ]
+    peaks = []
+    for d in range(1, others):
+        shift = [(i, (i + d) % others) for i in range(others)]
+        peaks.append(lax.ppermute(peak_out, "scen", shift))
     returned = returned.reshape(size.slots, 2 * scen)
-    args = [dst, returned, from_ahead, from_after, waves_out] + peaks
-    conv_state, wave_history, envelope = call(
-        functools.partial(end_kernel, size, len(peaks)),
+    conv_state, wave_history = call(
+        functools.partial(end_kernel, size),
         "end",
-        [hbm(conv_init.shape, F32), hbm(wave_init.shape, F32), hbm((1, size.nodes), F32)],
-        [HBM] * 3,
-        in_hbm(*args),
-        [HBM] * len(args),
+        [hbm(conv_init.shape, F32), hbm(wave_init.shape, F32)],
+        [HBM] * 2,
+        in_hbm(dst) + in_vmem(returned, from_ahead, from_after) + in_hbm(waves_out),
+        [HBM, VMEM, VMEM, VMEM, HBM],
         [
             vmem(dst.shape, I32),
-            vmem(returned.shape, F32),
             vmem((1, *size.drive), F32),
-            vmem((2, *size.exchange), F32),
-            vmem((others, 1, size.nodes), F32),
             vmem(conv_init.shape, F32),
-            vmem((1, size.nodes), F32),
-            dma((7 + others,)),
+            dma((3,)),
         ],
         16,
         {4: 1},
     )
+    envelope, conv_state = lax.optimization_barrier((peak_out, conv_state))
+    for peak in peaks:
+        envelope = jnp.maximum(envelope, peak)
     return voltage_out, branch_out, wave_history, conv_state, envelope.reshape(-1)
 
 

time: 106 us -> 91.3 us (0.86)
  Pallas kernels: 65.7 us -> 52.9 us
  local copies, waits for them, and re-layouts: 1.57 us -> 0 us
    pallas_call x11, Pallas kernels: 65.7 us -> 52.9 us  [call(): pl.pallas_call(kernel, name=name, out_shape=outs, in_specs=specs, out_spe...]
    all_to_all x1, waiting for transfers between devices: 0.01 us -> 3.01 us  [shards(): lax.all_to_all(packed, 'region', split_axis=0, concat_axis=0, tiled=True)]
    ppermute x3, waiting for transfers between devices: 3.16 us -> 0.44 us  [shards(): peaks.append(lax.ppermute(peak_out, 'scen', shift))]
    unnamed x14 -> x0, local copies, waits for them, and re-layouts: 1.57 us -> none
    max x0 -> x1, other arithmetic: none -> 1.33 us  [shards(): envelope = jnp.maximum(envelope, peak)]
    select_n x1 -> x0, other arithmetic: 1.33 us -> none  [shards(): jnp.where(first_row, conv_power[None, :], conv_node.astype(F32)[None, :])]
  transfers between devices with their start and end apart: 13 -> 13, of which waited for: 2 -> 4; matrix products, arithmetic and copies ran while one was open for 0% -> 0% of each run, Pallas kernels for 44% -> 43%
where the time goes in v3:
time: 91.3 us; the launch traced here: 90.8 us
  Pallas kernels  52.9 us (58%)
  starting transfers between devices  31.6 us (35%)
  waiting for transfers between devices  4.1 us (4%)
  other arithmetic  1.33 us (1%)
    pallas_call x11, Pallas kernels, call(): pl.pallas_call(kernel, name=name, out_shape=outs, in_specs=specs, out_spe...  52.9 us
    ppermute x4, starting transfers between devices, shards(): from_after = lax.ppermute(down, 'region', back_ring)  15.5 us
    all_to_all x1, starting transfers between devices, shards(): lax.all_to_all(packed, 'region', split_axis=0, concat_axis=0, tiled=True)  7.29 us
    ppermute x4, starting transfers between devices, shards(): from_ahead = lax.ppermute(up, 'region', ring)  3.56 us
    all_to_all x1, starting transfers between devices, shards(): lax.all_to_all(chunks, 'region', split_axis=0, concat_axis=0, tiled=True)  3.49 us
    all_to_all x1, waiting for transfers between devices, shards(): lax.all_to_all(packed, 'region', split_axis=0, concat_axis=0, tiled=True)  3.01 us
  transfers between devices with their start and end apart: 13, of which 4 were waited for; matrix products, arithmetic and copies ran while one was open for 0% of the time, Pallas kernels for 43%

profile of v3, /device:TPU:0, one launch (start us, length us, event | category | flops | bytes accessed | tf_op | source)
XLA Modules:
  0.0 90.8 jit_solution(7684912454396937982)
XLA Ops:
  0.6 3.0 %pack.1 = (f32[8,120,128]{2,1,0:T(8,128)}, s32[1,384]{1,0:T(1,128)}) custom-call(s32[1,384]{1,0:T(1,128)} %bitcast.26, f32[384]{0:T(512)} %power_hbm.1, s32[384]{0:T(512)} %node_hbm.1, f32[2,384]{1,0:T(2,128)} %gains_hbm.1, f32[2,64,384]{2,1,0:T(8,128)} %init_hbm.1), custom_call_target="tpu_custom_call" | custom-call | tf_op jit(solution)/shard_map/pack/pallas_call | solution.py:587
  3.7 7.3 %all-to-all-start = ((f32[8,120,128]{2,1,0:T(8,128)}), f32[8,120,128]{2,1,0:T(8,128)S(1)}, u32[]{:S(2)}, u32[]{:S(2)}) async-start(f32[8,120,128]{2,1,0:T(8,128)} %get-tuple-element.69), calls=%async_computation | async-start | bytes 983040 | tf_op jit(solution)/shard_map/all_to_all | solution.py:634
  11.0 10.8 %prep.1 = (bf16[32,480,256]{2,1,0:T(8,128)(2,1)}, bf16[4096,256]{1,0:T(8,128)(2,1)}, bf16[32,256,256]{2,1,0:T(8,128)(2,1)}, bf16[256,512]{1,0:T(8,128)(2,1)}, bf...) custom-call(s32[5,32]{1,0:T(8,128)} %bitcast.17, ...), custom_call_target="tpu_custom_call" | custom-call | tf_op jit(solution)/shard_map/prep/pallas_call | solution.py:587
  21.7 3.0 %all-to-all-done = f32[8,120,128]{2,1,0:T(8,128)S(1)} async-done(((f32[8,120,128]{2,1,0:T(8,128)}), f32[8,120,128]{2,1,0:T(8,128)S(1)}, u32[]{:S(2)}, u32[]{:S(2)}) %all-to-all-start) | async-done | bytes 491552 | tf_op jit(solution)/shard_map/all_to_all | solution.py:634
  24.7 9.9 %start.1 = (bf16[32,480,256]{2,1,0:T(8,128)(2,1)S(1)}, bf16[4096,256]{1,0:T(8,128)(2,1)S(1)}, bf16[32,256,256]{2,1,0:T(8,128)(2,1)S(1)}, bf16[256,512]{1,0:T(8,1...) custom-call(s32[5,32]{1,0:T(8,128)} %bitcast.18, ...), custom_call_target="tpu_custom_call" | custom-call | tf_op jit(solution)/shard_map/start/pallas_call | solution.py:587
  34.6 1.5 %collective-permute-start = (f32[64,128]{1,0:T(8,128)S(1)}, f32[64,128]{1,0:T(8,128)S(1)}, u32[]{:S(2)}, u32[]{:S(2)}) collective-permute-start(f32[64,128]{1,0:T(8,128)S(1)} %get-tuple-element.97), channel_id=1, source_target_pairs={{0,4},{4,8},{8,12},{12,16},{16,20},{20,24},{24,28},{28,0},{1,5},{5... | collective-permute-start | bytes 98312 | tf_op jit(solution)/shard_map/ppermute | solution.py:740
  36.1 3.3 %collective-permute-start.1 = (f32[64,128]{1,0:T(8,128)S(1)}, f32[64,128]{1,0:T(8,128)S(1)}, u32[]{:S(2)}, u32[]{:S(2)}) collective-permute-start(f32[64,128]{1,0:T(8,128)S(1)} %get-tuple-element.98), channel_id=1, source_target_pairs={{4,0},{8,4},{12,8},{16,12},{20,16},{24,20},{28,24},{0,28},{5,1},{9... | collective-permute-start | bytes 98312 | tf_op jit(solution)/shard_map/ppermute | solution.py:741
  39.4 6.9 %middle.3 = (f32[32,64,128]{2,1,0:T(8,128)S(1)}, f32[64,1024]{1,0:T(8,128)S(1)}, f32[64,1024]{1,0:T(8,128)S(1)}, f32[32,64,128]{2,1,0:T(8,128)S(1)}, f32[32,8,128]{2,1,0:T(8,128)S(1)}, /*index=5*/f32[64,256]{1,0:T(8,128)S(1)}) custom-call(s32[5,32]{1,0:T(8,128)} %bitcast.19, ...), custom_call_target="tpu_custom_call", output_to_operand_aliasing={{0}: (10, {}), {1}: (11, {}), {2}: (12, {}), {3}: (13, {}),... | custom-call | tf_op jit(solution)/shard_map/middle/pallas_call | solution.py:587
  46.3 0.2 launch.3
  46.5 0.1 collective-permute-start.2
  46.6 4.7 %collective-permute-start.3 = (f32[64,128]{1,0:T(8,128)S(1)}, f32[64,128]{1,0:T(8,128)S(1)}, u32[]{:S(2)}, u32[]{:S(2)}) collective-permute-start(f32[64,128]{1,0:T(8,128)S(1)} %get-tuple-element.107), channel_id=1, source_target_pairs={{4,0},{8,4},{12,8},{16,12},{20,16},{24,20},{28,24},{0,28},{5,1},{9... | collective-permute-start | bytes 98312 | tf_op jit(solution)/shard_map/ppermute | solution.py:741
  51.3 6.9 %middle.4 = (f32[32,64,128]{2,1,0:T(8,128)S(1)}, f32[64,1024]{1,0:T(8,128)S(1)}, f32[64,1024]{1,0:T(8,128)S(1)}, f32[32,64,128]{2,1,0:T(8,128)S(1)}, f32[32,8,128]{2,1,0:T(8,128)S(1)}, /*index=5*/f32[64,256]{1,0:T(8,128)S(1)}) custom-call(s32[5,32]{1,0:T(8,128)} %bitcast.20, ...), custom_call_target="tpu_custom_call", output_to_operand_aliasing={{0}: (10, {}), {1}: (11, {}), {2}: (12, {}), {3}: (13, {}),... | custom-call | tf_op jit(solution)/shard_map/middle/pallas_call | solution.py:587
  58.2 0.0 collective-permute-done.2.refs_0_.refs_2_
  58.2 0.0 collective-permute-done.3.refs_1_.refs_3_
  58.2 0.2 launch.4
  58.4 0.1 collective-permute-start.4
  58.5 4.7 %collective-permute-start.5 = (f32[64,128]{1,0:T(8,128)S(1)}, f32[64,128]{1,0:T(8,128)S(1)}, u32[]{:S(2)}, u32[]{:S(2)}) collective-permute-start(f32[64,128]{1,0:T(8,128)S(1)} %get-tuple-element.116), channel_id=1, source_target_pairs={{4,0},{8,4},{12,8},{16,12},{20,16},{24,20},{28,24},{0,28},{5,1},{9... | collective-permute-start | bytes 98312 | tf_op jit(solution)/shard_map/ppermute | solution.py:741
  63.2 7.7 %middle.5 = (f32[32,64,128]{2,1,0:T(8,128)S(1)}, f32[64,1024]{1,0:T(8,128)S(1)}, f32[64,1024]{1,0:T(8,128)S(1)}, f32[32,64,128]{2,1,0:T(8,128)S(1)}, f32[32,8,12...) custom-call(s32[5,32]{1,0:T(8,128)} %bitcast.21, ...), custom_call_target="tpu_custom_call", output_to_operand_aliasing={{0}: (10, {}), {1}: (11, {}), {2}: (12, {}), {3}: (13, {}),... | custom-call | tf_op jit(solution)/shard_map/middle/pallas_call | solution.py:587
  71.0 0.0 collective-permute-done.4.refs_0_
  71.0 1.0 %launch.5 = (f32[64,256]{1,0:T(8,128)}, f32[64,128]{1,0:T(8,128)S(1)}, f32[64,128]{1,0:T(8,128)S(1)}, f32[960,128]{1,0:T(8,128)}, f32[8,64,256]{2,1,0:T(8,128)}) custom-call(f32[64,256]{1,0:T(8,128)S(1)} %get-tuple-element.114.at_ends, bf16[256,512]{1,0:T(8,128)(2,1)S(1)} %get-tuple-element.94.kk, f32[8,256]{1,0:T(8,128)S(1)} %get-tuple-element.95.ends, ...), custom_call_target="tpu_custom_call" | custom-call | tf_op jit(solution)/shard_map/launch/pallas_call | solution.py:587
  72.0 3.5 %all-to-all-start.1 = ((f32[8,120,128]{2,1,0:T(8,128)}), f32[8,120,128]{2,1,0:T(8,128)S(1)}, u32[]{:S(2)}, u32[]{:S(2)}) async-start(f32[8,120,128]{2,1,0:T(8,128)} %bitcast.16), calls=%async_computation.1 | async-start | bytes 983040 | tf_op jit(solution)/shard_map/all_to_all | solution.py:802
  75.5 1.9 %collective-permute-start.6 = (f32[64,128]{1,0:T(8,128)S(1)}, f32[64,128]{1,0:T(8,128)S(1)}, u32[]{:S(2)}, u32[]{:S(2)}) collective-permute-start(f32[64,128]{1,0:T(8,128)S(1)} %get-tuple-element.125), channel_id=1, source_target_pairs={{0,4},{4,8},{8,12},{12,16},{16,20},{20,24},{24,28},{28,0},{1,5},{5... | collective-permute-start | bytes 98312 | tf_op jit(solution)/shard_map/ppermute | solution.py:799
  77.4 2.9 %collective-permute-start.7 = (f32[64,128]{1,0:T(8,128)S(1)}, f32[64,128]{1,0:T(8,128)S(1)}, u32[]{:S(2)}, u32[]{:S(2)}) collective-permute-start(f32[64,128]{1,0:T(8,128)S(1)} %get-tuple-element.126), channel_id=1, source_target_pairs={{4,0},{8,4},{12,8},{16,12},{20,16},{24,20},{28,24},{0,28},{5,1},{9... | collective-permute-start | bytes 98312 | tf_op jit(solution)/shard_map/ppermute | solution.py:800
  80.2 4.3 %final.1 = (f32[64,3072]{1,0:T(8,128)}, f32[1,3072]{1,0:T(1,128)}) custom-call(f32[64,256]{1,0:T(8,128)} %get-tuple-element.118.drive_hbm, f32[32,64,128]{2,1,0:T(8,128)} %get-tuple-element.119.volt_hbm, bf16[32,256,256]{2,1,0:T(8,128)(2,1)} %get-tuple-element.72.mt_hbm, f32[32,8,128]{2,1,0:T(8,128)} %get-tuple-element.120.peak_hbm), custom_call_target="tpu_custom_call" | custom-call | tf_op jit(solution)/shard_map/final/pallas_call | solution.py:587
  84.6 0.1 collective-permute-start.10
  84.6 1.6 %collective-permute-start.9 = (f32[1,3072]{1,0:T(1,128)}, f32[1,3072]{1,0:T(1,128)S(1)}, u32[]{:S(2)}, u32[]{:S(2)}) collective-permute-start(f32[1,3072]{1,0:T(1,128)} %get-tuple-element.132), channel_id=1, source_target_pairs={{0,2},{1,3},{2,0},{3,1},{4,6},{5,7},{6,4},{7,5},{8,10},{9,11},{10,... | collective-permute-start | bytes 36872 | tf_op jit(solution)/shard_map/ppermute | solution.py:825
  86.2 0.2 collective-permute-start.8
  86.3 0.3 collective-permute-done.6.ahead
  86.7 0.3 all-to-all-done.1
  87.0 2.1 %end.1 = (f32[2,64,384]{2,1,0:T(8,128)}, f32[8,64,256]{2,1,0:T(8,128)}) custom-call(s32[1,384]{1,0:T(1,128)} %get-tuple-element.123.dst_hbm, f32[960,128]{1,0:T(8,128)S(1)} %bitcast.14, f32[64,128]{1,0:T(8,128)S(1)} %collective-permute-done.6.ahead, f32[64,128]{1,0:T(8,128)S(1)} %collective-permute-done.7.after, ...), custom_call_target="tpu_custom_call", output_to_operand_aliasing={{1}: (4, {})} | custom-call | tf_op jit(solution)/shard_map/end/pallas_call | solution.py:587
  89.1 0.4 collective-permute-done.8
  89.5 1.3 %maximum_maximum_fusion = f32[1,3072]{1,0:T(1,128)} fusion(f32[1,3072]{1,0:T(1,128)S(1)} %collective-permute-done.10, f32[1,3072]{1,0:T(1,128)S(1)} %collective-permute-done.9, f32[1,3072]{1,0:T(1,128)} %get-tuple-element.132, f32[1,3072]{1,0:T(1,128)S(1)} %collective-permute-done.8), kind=kLoop, calls=%fused_computation | loop fusion | flops 9216 | bytes 61440 | tf_op jit(solution)/shard_map/max | solution.py:845
  (6 shorter events, 0.0 us)
Async XLA Ops:
  3.7 21.1 %all-to-all-start = ((f32[8,120,128]{2,1,0:T(8,128)}), f32[8,120,128]{2,1,0:T(8,128)S(1)}, u32[]{:S(2)}, u32[]{:S(2)}) async-start(f32[8,120,128]{2,1,0:T(8,128)} %get-tuple-element.69), calls=%async_computation | async-start | bytes 983040 | tf_op jit(solution)/shard_map/all_to_all | solution.py:634
  34.6 11.7 %collective-permute-start = (f32[64,128]{1,0:T(8,128)S(1)}, f32[64,128]{1,0:T(8,128)S(1)}, u32[]{:S(2)}, u32[]{:S(2)}) collective-permute-start(f32[64,128]{1,0:T(8,128)S(1)} %get-tuple-element.97), channel_id=1, source_target_pairs={{0,4},{4,8},{8,12},{12,16},{16,20},{20,24},{24,28},{28,0},{1,5},{5... | collective-permute-start | bytes 98312 | tf_op jit(solution)/shard_map/ppermute | solution.py:740
  36.1 10.2 %collective-permute-start.1 = (f32[64,128]{1,0:T(8,128)S(1)}, f32[64,128]{1,0:T(8,128)S(1)}, u32[]{:S(2)}, u32[]{:S(2)}) collective-permute-start(f32[64,128]{1,0:T(8,128)S(1)} %get-tuple-element.98), channel_id=1, source_target_pairs={{4,0},{8,4},{12,8},{16,12},{20,16},{24,20},{28,24},{0,28},{5,1},{9... | collective-permute-start | bytes 98312 | tf_op jit(solution)/shard_map/ppermute | solution.py:741
  46.5 11.7 %collective-permute-start.2 = (f32[64,128]{1,0:T(8,128)S(1)}, f32[64,128]{1,0:T(8,128)S(1)}, u32[]{:S(2)}, u32[]{:S(2)}) collective-permute-start(f32[64,128]{1,0:T(8,128)S(1)} %get-tuple-element.106), channel_id=1, source_target_pairs={{0,4},{4,8},{8,12},{12,16},{16,20},{20,24},{24,28},{28,0},{1,5},{5... | collective-permute-start | bytes 98312 | tf_op jit(solution)/shard_map/ppermute | solution.py:740
  46.6 11.6 %collective-permute-start.3 = (f32[64,128]{1,0:T(8,128)S(1)}, f32[64,128]{1,0:T(8,128)S(1)}, u32[]{:S(2)}, u32[]{:S(2)}) collective-permute-start(f32[64,128]{1,0:T(8,128)S(1)} %get-tuple-element.107), channel_id=1, source_target_pairs={{4,0},{8,4},{12,8},{16,12},{20,16},{24,20},{28,24},{0,28},{5,1},{9... | collective-permute-start | bytes 98312 | tf_op jit(solution)/shard_map/ppermute | solution.py:741
  58.4 12.5 %collective-permute-start.4 = (f32[64,128]{1,0:T(8,128)S(1)}, f32[64,128]{1,0:T(8,128)S(1)}, u32[]{:S(2)}, u32[]{:S(2)}) collective-permute-start(f32[64,128]{1,0:T(8,128)S(1)} %get-tuple-element.115), channel_id=1, source_target_pairs={{0,4},{4,8},{8,12},{12,16},{16,20},{20,24},{24,28},{28,0},{1,5},{5... | collective-permute-start | bytes 98312 | tf_op jit(solution)/shard_map/ppermute | solution.py:740
  58.5 12.5 %collective-permute-start.5 = (f32[64,128]{1,0:T(8,128)S(1)}, f32[64,128]{1,0:T(8,128)S(1)}, u32[]{:S(2)}, u32[]{:S(2)}) collective-permute-start(f32[64,128]{1,0:T(8,128)S(1)} %get-tuple-element.116), channel_id=1, source_target_pairs={{4,0},{8,4},{12,8},{16,12},{20,16},{24,20},{28,24},{0,28},{5,1},{9... | collective-permute-start | bytes 98312 | tf_op jit(solution)/shard_map/ppermute | solution.py:741
  72.0 15.0 %all-to-all-start.1 = ((f32[8,120,128]{2,1,0:T(8,128)}), f32[8,120,128]{2,1,0:T(8,128)S(1)}, u32[]{:S(2)}, u32[]{:S(2)}) async-start(f32[8,120,128]{2,1,0:T(8,128)} %bitcast.16), calls=%async_computation.1 | async-start | bytes 983040 | tf_op jit(solution)/shard_map/all_to_all | solution.py:802
  75.5 11.2 %collective-permute-start.6 = (f32[64,128]{1,0:T(8,128)S(1)}, f32[64,128]{1,0:T(8,128)S(1)}, u32[]{:S(2)}, u32[]{:S(2)}) collective-permute-start(f32[64,128]{1,0:T(8,128)S(1)} %get-tuple-element.125), channel_id=1, source_target_pairs={{0,4},{4,8},{8,12},{12,16},{16,20},{20,24},{24,28},{28,0},{1,5},{5... | collective-permute-start | bytes 98312 | tf_op jit(solution)/shard_map/ppermute | solution.py:799
  77.4 9.3 %collective-permute-start.7 = (f32[64,128]{1,0:T(8,128)S(1)}, f32[64,128]{1,0:T(8,128)S(1)}, u32[]{:S(2)}, u32[]{:S(2)}) collective-permute-start(f32[64,128]{1,0:T(8,128)S(1)} %get-tuple-element.126), channel_id=1, source_target_pairs={{4,0},{8,4},{12,8},{16,12},{20,16},{24,20},{28,24},{0,28},{5,1},{9... | collective-permute-start | bytes 98312 | tf_op jit(solution)/shard_map/ppermute | solution.py:800
  84.6 4.5 %collective-permute-start.10 = (f32[1,3072]{1,0:T(1,128)}, f32[1,3072]{1,0:T(1,128)S(1)}, u32[]{:S(2)}, u32[]{:S(2)}) collective-permute-start(f32[1,3072]{1,0:T(1,128)} %get-tuple-element.132), channel_id=1, source_target_pairs={{0,3},{1,0},{2,1},{3,2},{4,7},{5,4},{6,5},{7,6},{8,11},{9,8},{10,9... | collective-permute-start | bytes 36872 | tf_op jit(solution)/shard_map/ppermute | solution.py:825
  84.6 4.4 %collective-permute-start.9 = (f32[1,3072]{1,0:T(1,128)}, f32[1,3072]{1,0:T(1,128)S(1)}, u32[]{:S(2)}, u32[]{:S(2)}) collective-permute-start(f32[1,3072]{1,0:T(1,128)} %get-tuple-element.132), channel_id=1, source_target_pairs={{0,2},{1,3},{2,0},{3,1},{4,6},{5,7},{6,4},{7,5},{8,10},{9,11},{10,... | collective-permute-start | bytes 36872 | tf_op jit(solution)/shard_map/ppermute | solution.py:825
  86.2 3.3 %collective-permute-start.8 = (f32[1,3072]{1,0:T(1,128)}, f32[1,3072]{1,0:T(1,128)S(1)}, u32[]{:S(2)}, u32[]{:S(2)}) collective-permute-start(f32[1,3072]{1,0:T(1,128)} %get-tuple-element.132), channel_id=1, source_target_pairs={{0,1},{1,2},{2,3},{3,0},{4,5},{5,6},{6,7},{7,4},{8,9},{9,10},{10,1... | collective-permute-start | bytes 36872 | tf_op jit(solution)/shard_map/ppermute | solution.py:825
